TPU v7x, 256 devices: a whole 4x4x8 slice. The times are simulated.
256 devices in a mesh: tm: 16 (over y, z_hi), space: 16 (over x, z_lo, core).
Axes of the slice: x: 4, y: 4, z: 8 (z_hi: 4, z_lo: 2; z = z_hi * 2 + z_lo), core: 2. Of those that a mesh axis runs over, the one named last changes fastest.
Arguments:
- tokens: bfloat16 [32, 16, 4, 49, 1408], P('tm', 'space'), may hold values from -6 to 6
- tile_of_slot: int32 [16], replicated, may hold values from 0 to 15, each once
- shifts: int32 [4, 2], replicated, may hold values from 0 to 13
- norm_gain_space: float32 [1408], replicated, may hold values from 0.1 to 1.9
- norm_bias_space: float32 [1408], replicated, may hold values from -3 to 3
- w_qkv_space: bfloat16 [1408, 3168], P('tm'), may hold values from -0.15625 to 0.15625
- w_out_space: bfloat16 [1056, 1408], P(None, 'tm'), may hold values from -0.1875 to 0.1875
- norm_gain_time: float32 [1408], replicated, may hold values from 0.1 to 1.9
- norm_bias_time: float32 [1408], replicated, may hold values from -3 to 3
- w_qkv_time: bfloat16 [1408, 3168], P('tm'), may hold values from -0.15625 to 0.15625
- w_out_time: bfloat16 [1056, 1408], P(None, 'tm'), may hold values from -0.1875 to 0.1875
Outputs:
- encoded: bfloat16 [32, 16, 4, 49, 1408], P('tm', 'space')
Inputs may be any that keep to these rules, and one draw needn't show every extreme that they name: `tile_of_slot`: each of the 16 tiles is held by exactly one slot. `shifts`: offsets of a video's cyclic window shift, rows first.
All inputs are finite; a program needn't handle non-finite values.
Results may differ from a plain program's by a relative error of at most 0.012.
Values may be sent and summed in bfloat16 or wider, within the bound.
A program may use at most 128 MiB of HBM per device.

v0:
```python
import math

import jax
import jax.numpy as jnp
from jax import lax
from jax.sharding import PartitionSpec as P

HEADS = 12
HEAD_DIM = 88
TILE = 7
WINDOW = 14


EPSILON = 1e-06


def layer_norm(values, norm_gain, norm_bias):
    widened = values.astype(jnp.float32)
    average = jnp.mean(widened, axis=-1, keepdims=True)
    centered = widened - average
    variance = jnp.mean(centered * centered, axis=-1, keepdims=True)
    return (centered * lax.rsqrt(variance + EPSILON) * norm_gain + norm_bias).astype(jnp.bfloat16)


def project(values, weight):
    flattened = values.reshape(-1, values.shape[-1])
    return jnp.dot(flattened, weight, preferred_element_type=jnp.float32).reshape(
        values.shape[:-1] + (weight.shape[1],)
    )


def project_bf(values, weight):
    return project(values, weight).astype(jnp.bfloat16)


def window_attend(frame_cells, offsets):
    frame_side = frame_cells.shape[0]
    head_count = frame_cells.shape[-1] // (3 * HEAD_DIM)
    per_side = frame_side // WINDOW
    places = jnp.arange(frame_side, dtype=jnp.int32)
    row_index = (places + offsets[0]) % frame_side
    col_index = (places + offsets[1]) % frame_side
    rolled = jnp.take(jnp.take(frame_cells, row_index, axis=0), col_index, axis=1)
    pieces = rolled.reshape(per_side, WINDOW, per_side, WINDOW, 3, head_count, HEAD_DIM)
    pieces = pieces.transpose(4, 0, 2, 5, 1, 3, 6).reshape(
        3, per_side * per_side, head_count, WINDOW * WINDOW, HEAD_DIM
    )
    row_part = (places >= frame_side - offsets[0]).astype(jnp.int32)
    col_part = (places >= frame_side - offsets[1]).astype(jnp.int32)
    region = (2 * row_part[:, None] + col_part[None, :]).reshape(per_side, WINDOW, per_side, WINDOW)
    region = region.transpose(0, 2, 1, 3).reshape(per_side * per_side, WINDOW * WINDOW)
    allowed = region[:, :, None] == region[:, None, :]
    scores = jnp.einsum(
        "whqd,whkd->whqk", pieces[0], pieces[1], preferred_element_type=jnp.float32
    ) * HEAD_DIM ** (-0.5)
    weights = jnp.where(allowed[:, None], jnp.exp(scores), jnp.float32(0.0))
    shares = (weights / jnp.sum(weights, axis=-1, keepdims=True)).astype(jnp.bfloat16)
    attended = jnp.einsum(
        "whqk,whkd->whqd", shares, pieces[2], preferred_element_type=jnp.float32
    ).astype(jnp.bfloat16)
    attended = attended.reshape(per_side, per_side, head_count, WINDOW, WINDOW, HEAD_DIM)
    attended = attended.transpose(0, 3, 1, 4, 2, 5).reshape(
        frame_side, frame_side, head_count * HEAD_DIM
    )
    back_rows = (places - offsets[0]) % frame_side
    back_cols = (places - offsets[1]) % frame_side
    return jnp.take(jnp.take(attended, back_rows, axis=0), back_cols, axis=1)


def time_attend(packed):
    leading = packed.shape[:-1]
    pieces = packed.reshape(leading[0], -1, 3, HEADS, HEAD_DIM)
    scores = jnp.einsum(
        "tmhd,umhd->mhtu", pieces[:, :, 0], pieces[:, :, 1], preferred_element_type=jnp.float32
    ) * HEAD_DIM ** (-0.5)
    weights = jnp.exp(scores)
    shares = (weights / jnp.sum(weights, axis=-1, keepdims=True)).astype(jnp.bfloat16)
    attended = jnp.einsum(
        "mhtu,umhd->tmhd", shares, pieces[:, :, 2], preferred_element_type=jnp.float32
    ).astype(jnp.bfloat16)
    return attended.reshape(leading + (HEADS * HEAD_DIM,))


def body(
    tokens,
    tile_of_slot,
    shifts,
    norm_gain_space,
    norm_bias_space,
    w_qkv_space,
    w_out_space,
    norm_gain_time,
    norm_bias_time,
    w_qkv_time,
    w_out_time,
):
    qkv_space, out_space, qkv_time, out_time = (
        lax.all_gather(w_qkv_space, "tm", axis=0, tiled=True),
        lax.all_gather(w_out_space, "tm", axis=1, tiled=True),
        lax.all_gather(w_qkv_time, "tm", axis=0, tiled=True),
        lax.all_gather(w_out_time, "tm", axis=1, tiled=True),
    )
    local_steps = tokens.shape[0]
    video_count = tokens.shape[2]
    per_tile = tokens.shape[3]
    width = tokens.shape[4]
    frame_count = local_steps * video_count
    own_tokens = tokens.reshape(frame_count, per_tile, width)
    slot_count = lax.axis_size("space")
    side_tiles = math.isqrt(slot_count)
    frame_side = TILE * side_tiles
    group_heads = max(1, slot_count // frame_count)
    normed = layer_norm(own_tokens, norm_gain_space, norm_bias_space)
    projected = project_bf(normed, qkv_space)
    payload = projected.reshape(frame_count, per_tile, 3, group_heads, -1).transpose(0, 3, 1, 2, 4)
    payload = payload.reshape(frame_count * group_heads, per_tile, -1)
    arrived = lax.all_to_all(payload[None], "space", split_axis=1, concat_axis=0, tiled=True)
    per_device = arrived.shape[1]
    first_entry = lax.axis_index("space") * per_device
    entries = first_entry + jnp.arange(per_device, dtype=jnp.int32)
    positions = jnp.arange(slot_count, dtype=jnp.int32)
    inverse = jnp.sum(
        jnp.where(tile_of_slot[None, :] == positions[:, None], positions[None, :], 0), axis=1
    )
    tile_grid = jnp.take(arrived, inverse, axis=0).reshape(
        side_tiles, side_tiles, per_device, TILE, TILE, -1
    )
    frame_grid = tile_grid.transpose(2, 0, 3, 1, 4, 5).reshape(
        per_device, frame_side, frame_side, -1
    )
    video_ids = entries // group_heads % video_count
    own_shifts = jnp.take(shifts, video_ids, axis=0)
    attended = jax.vmap(window_attend)(frame_grid, own_shifts)
    back_tiles = attended.reshape(per_device, side_tiles, TILE, side_tiles, TILE, -1)
    back_tiles = back_tiles.transpose(1, 3, 0, 2, 4, 5).reshape(
        slot_count, per_device, TILE * TILE, -1
    )
    back_slots = jnp.take(back_tiles, tile_of_slot, axis=0)
    returned = lax.all_to_all(back_slots, "space", split_axis=0, concat_axis=1, tiled=True)
    mixed = (
        returned[0]
        .reshape(frame_count, group_heads, per_tile, -1)
        .transpose(0, 2, 1, 3)
        .reshape(frame_count, per_tile, -1)
    )
    middle = (own_tokens.astype(jnp.float32) + project(mixed, out_space)).astype(jnp.bfloat16)
    normed_time = layer_norm(middle, norm_gain_time, norm_bias_time)
    payload_time = project_bf(normed_time, qkv_time)
    group_count = lax.axis_size("tm")
    row_count = video_count * per_tile
    row_share = -(-row_count // group_count)
    padded_rows = row_share * group_count
    flat_rows = payload_time.reshape(local_steps, row_count, -1)
    flat_rows = jnp.pad(flat_rows, ((0, 0), (0, padded_rows - row_count), (0, 0)))
    grouped = flat_rows.reshape(local_steps, group_count, row_share, -1)
    result = lax.all_to_all(
        time_attend(lax.all_to_all(grouped, "tm", split_axis=1, concat_axis=0, tiled=True)),
        "tm",
        split_axis=0,
        concat_axis=1,
        tiled=True,
    )
    result = result.reshape(local_steps, padded_rows, -1)[:, :row_count]
    result = result.reshape(frame_count, per_tile, -1)
    outcome = (middle.astype(jnp.float32) + project(result, out_time)).astype(jnp.bfloat16)
    return outcome.reshape(tokens.shape)


def solution(mesh):
    placed = (
        P("tm", "space", None, None, None),
        P(),
        P(),
        P(),
        P(),
        P("tm", None),
        P(None, "tm"),
        P(),
        P(),
        P("tm", None),
        P(None, "tm"),
    )
    return jax.shard_map(
        body,
        mesh=mesh,
        in_specs=placed,
        out_specs=P("tm", "space", None, None, None),
        check_vma=False,
    )
```

profile of v0, /device:TPU:35, one launch (start us, length us, event | category | flops | bytes accessed | tf_op | source)
XLA Modules:
  0.0 526.9 jit_solution(8736569242402285264)
XLA Ops:
  15.0 120.6 %all-gather.5.cloned.1.call-done = bf16[1408,3168]{1,0:T(8,128)(2,1)} async-done(((bf16[88,3168]{1,0:T(8,128)(2,1)}), bf16[1408,3168]{1,0:T(8,128)(2,1)}) %all-gather.5.cloned.1.call-update) | async-done | bytes 8921104 | tf_op jit(solution)/shard_map/all_gather | solution.py:98
  135.6 10.4 %fusion.4 = bf16[8,49,3168]{2,1,0:T(8,128)(2,1)} fusion(bf16[8,49,1408]{2,1,0:T(8,128)(2,1)} %fusion.36, bf16[1408,3168]{1,0:T(8,128)(2,1)} %all-gather.5.cloned.1.call-done), kind=kOutput, calls=%fused_computation.10 | convolution fusion | flops 3498308352 | bytes 12508672 | tf_op jit(solution)/shard_map/dot_general | solution.py:27
  145.9 6.6 %reshape.684 = bf16[8,49,3,2,528]{4,3,2,1,0:T(2,128)(2,1)S(1)} reshape(bf16[8,49,3168]{2,1,0:T(8,128)(2,1)} %fusion.4) | data formatting | bytes 4967424 | tf_op jit(solution)/shard_map/reshape | solution.py:115
  152.5 3.5 copy.226
  156.1 7.7 %reshape.685 = bf16[1,16,49,1584]{3,2,0,1:T(8,128)(2,1)} reshape(bf16[8,2,49,3,528]{4,3,2,1,0:T(4,128)(2,1)} %copy.226) | data formatting | bytes 4967424 | tf_op jit(solution)/shard_map/broadcast_in_dim;reshape | solution.py:117
  163.8 6.3 %all-to-all-start = ((bf16[1,16,49,1584]{3,2,0,1:T(8,128)(2,1)}), bf16[1,16,49,1584]{3,2,0,1:T(8,128)(2,1)S(1)}, u32[]{:S(2)}, u32[]{:S(2)}) async-start(bf16[1,16,49,1584]{3,2,0,1:T(8,128)(2,1)} %reshape.685), calls=%async_computation | async-start | bytes 5963776 | tf_op jit(solution)/shard_map/all_to_all | solution.py:117
  176.9 52.5 %all-to-all-done = bf16[1,16,49,1584]{3,2,0,1:T(8,128)(2,1)S(1)} async-done(((bf16[1,16,49,1584]{3,2,0,1:T(8,128)(2,1)}), bf16[1,16,49,1584]{3,2,0,1:T(8,128)(2,1)S(1)}, u32[]{:S(2)}, u32[]{:S(2)}) %all-to-all-start) | async-done | bytes 2483744 | tf_op jit(solution)/shard_map/all_to_all | solution.py:117
  231.8 4.2 reshape.686
  238.0 2.9 reshape.581
  240.9 2.8 gather_fusion.2
  250.1 6.7 %gather.39 = bf16[1,2,14,2,14,3,6,88]{7,6,5,4,3,2,1,0:T(8,128)(2,1)} reshape(bf16[28,28,1584]{2,1,0:T(8,128)(2,1)S(1)} %copy.195) | data formatting | bytes 4967424 | tf_op jit(solution)/shard_map/vmap(jit(_take))/gather | solution.py:43
  256.8 3.0 select_bitcast_fusion
  259.8 2.8 copy.196
  282.4 61.9 %all_to_all.51 = bf16[16,1,49,528]{3,2,1,0:T(8,128)(2,1)S(1)} all-to-all(bf16[16,1,49,528]{3,2,1,0:T(8,128)(2,1)S(1)} %fusion.48), channel_id=1, replica_groups=mesh['tm'=16,'space'=16] {'space'}, dimensions={0} | all-to-all | bytes 1655808 | tf_op jit(solution)/shard_map/all_to_all | solution.py:139
  346.5 4.2 convert_reduce_fusion
  352.9 10.7 %fusion.7 = bf16[8,49,3168]{2,1,0:T(8,128)(2,1)} fusion(bf16[1408,3168]{1,0:T(8,128)(2,1)} %all-gather.9.cloned.1.call-done, bf16[8,49,1408]{2,1,0:T(8,128)(2,1)} %copy-done.3, f32[1408]{0:T(1024)S(1)} %copy-done.9, f32[1408]{0:T(1024)S(1)} %copy-done.10, f32[8,49]{1,0:T(8,128)S(1)} %add_rsqrt_fusion.1, f32[8,49]{1,0:T(8,128)S(1)} %broadcast_multiply_fusion.1), kind=kOutput, calls=%fused_computation.11 | convolution fusion | flops 3501619968 | bytes 12523072 | tf_op jit(solution)/shard_map/dot_general | solution.py:27
  368.1 3.5 pad.4.clone
  371.6 6.7 %all-to-all-start.2 = ((bf16[2,16,13,3168]{3,0,2,1:T(2,128)(2,1)}), bf16[2,16,13,3168]{3,0,2,1:T(2,128)(2,1)S(1)}, u32[]{:S(2)}, u32[]{:S(2)}) async-start(bf16[2,16,13,3168]{3,0,2,1:T(2,128)(2,1)} %bitcast.44), calls=%async_computation.2 | async-start | bytes 5324800 | tf_op jit(solution)/shard_map/all_to_all | solution.py:157
  378.9 67.2 %all-to-all-done.2 = bf16[2,16,13,3168]{3,0,2,1:T(2,128)(2,1)S(1)} async-done(((bf16[2,16,13,3168]{3,0,2,1:T(2,128)(2,1)}), bf16[2,16,13,3168]{3,0,2,1:T(2,128)(2,1)S(1)}, u32[]{:S(2)}, u32[]{:S(2)}) %all-to-all-start.2) | async-done | bytes 2635808 | tf_op jit(solution)/shard_map/all_to_all | solution.py:157
  446.1 3.4 copy.211
  449.5 10.8 %reshape.591 = bf16[32,13,3,12,88]{4,3,2,0,1:T(8,128)(2,1)} reshape(bf16[16,2,1,13,3168]{4,1,0,3,2:T(2,128)(2,1)} %copy.211) | data formatting | bytes 5271552 | tf_op jit(solution)/shard_map/reshape | solution.py:72
  460.3 3.4 fusion.62
  468.3 43.6 %all_to_all.52 = bf16[32,1,13,1056]{3,2,1,0:T(8,128)(2,1)S(1)} all-to-all(bf16[32,1,13,1056]{3,2,1,0:T(8,128)(2,1)S(1)} %reshape.689), channel_id=1, replica_groups=mesh['tm'=16,'space'=16] {'tm'}, dimensions={0} | all-to-all | bytes 1757184 | tf_op jit(solution)/shard_map/all_to_all | solution.py:156
  514.7 3.9 fusion.22
  (114 shorter events, 62.0 us)
Async XLA Ops:
  6.5 129.0 %all-gather.5.cloned.1.call-start = ((), (), s32[]{:S(2)}) async-start(), calls=%async_computation.4 | async-start | bytes 9574400 | tf_op jit(solution)/shard_map/all_gather | solution.py:98
  7.3 339.3 %all-gather.7.cloned.1.call-start = ((), (), s32[]{:S(2)}) async-start(), calls=%async_computation.5 | async-start | bytes 3446784 | tf_op jit(solution)/shard_map/all_gather | solution.py:99
  8.0 344.9 %all-gather.9.cloned.1.call-start = ((), (), s32[]{:S(2)}) async-start(), calls=%async_computation.6 | async-start | bytes 9574400 | tf_op jit(solution)/shard_map/all_gather | solution.py:100
  8.7 1.6 copy-start.2
  8.8 4.7 copy-start.6
  8.8 4.7 copy-start.7
  10.3 4.7 copy-start
  163.8 6.4 %copy-start.11 = (s32[16]{0:T(128)S(1)}, s32[16]{0:T(128)}, u32[]{:S(2)}) copy-start(s32[16]{0:T(128)} %param.12) | copy-start | bytes 196
  163.8 6.6 %copy-start.8 = (s32[4,2]{0,1:T(2,128)S(1)}, s32[4,2]{0,1:T(2,128)}, u32[]{:S(2)}) copy-start(s32[4,2]{0,1:T(2,128)} %param.13) | copy-start | bytes 100
  163.8 65.6 %all-to-all-start = ((bf16[1,16,49,1584]{3,2,0,1:T(8,128)(2,1)}), bf16[1,16,49,1584]{3,2,0,1:T(8,128)(2,1)S(1)}, u32[]{:S(2)}, u32[]{:S(2)}) async-start(bf16[1,16,49,1584]{3,2,0,1:T(8,128)(2,1)} %reshape.685), calls=%async_computation | async-start | bytes 5963776 | tf_op jit(solution)/shard_map/all_to_all | solution.py:117
  270.6 2.8 copy-start.5
  344.2 2.3 copy-start.1
  346.5 6.3 %copy-start.9 = (f32[1408]{0:T(1024)S(1)}, f32[1408]{0:T(1024)}, u32[]{:S(2)}) copy-start(f32[1408]{0:T(1024)} %param.19) | copy-start | bytes 16900
  346.5 6.3 %copy-start.10 = (f32[1408]{0:T(1024)S(1)}, f32[1408]{0:T(1024)}, u32[]{:S(2)}) copy-start(f32[1408]{0:T(1024)} %param.18) | copy-start | bytes 16900
  350.8 1.1 copy-start.3
  371.6 74.5 %all-to-all-start.2 = ((bf16[2,16,13,3168]{3,0,2,1:T(2,128)(2,1)}), bf16[2,16,13,3168]{3,0,2,1:T(2,128)(2,1)S(1)}, u32[]{:S(2)}, u32[]{:S(2)}) async-start(bf16[2,16,13,3168]{3,0,2,1:T(2,128)(2,1)} %bitcast.44), calls=%async_computation.2 | async-start | bytes 5324800 | tf_op jit(solution)/shard_map/all_to_all | solution.py:157
  378.4 136.2 %all-gather.11.cloned.1.call-start = ((), (), s32[]{:S(2)}) async-start(), calls=%async_computation.7 | async-start | bytes 3446784 | tf_op jit(solution)/shard_map/all_gather | solution.py:101
  513.4 1.3 copy-start.4
Sparse Core Ops, SparseCore 0:
  9.8 125.6 all-gather.4
  138.0 78.8 all-gather.6
  219.4 133.3 all-gather.8
  381.4 109.2 all-gather.10
where the time goes:
time: 537 us; the launch traced here: 527 us
  waiting for transfers between devices  243 us (45%)
  blocking collectives  105 us (20%)
  local copies, waits for them, and re-layouts  99.3 us (18%)
  matrix products  35 us (7%)
  between operations  15.4 us (3%)
  other arithmetic  15.1 us (3%)
  starting transfers between devices  13.2 us (2%)
    all_gather x1, waiting for transfers between devices, body(): lax.all_gather(w_qkv_space, 'tm', axis=0, tiled=True)  121 us
    all_to_all x1, waiting for transfers between devices, body(): lax.all_to_all(grouped, 'tm', split_axis=1, concat_axis=0, tiled=True)  67.2 us
    all_to_all x1, blocking collectives, body(): lax.all_to_all(back_slots, 'space', split_axis=0, concat_axis=1, tiled=True)  61.9 us
    all_to_all x1, waiting for transfers between devices, body(): lax.all_to_all(payload[None], 'space', split_axis=1, concat_axis=0, tiled...  52.5 us
    all_to_all x1, blocking collectives, body(): lax.all_to_all(time_attend(lax.all_to_all(grouped, 'tm', split_axis=1, co...  43.6 us
    dot_general x4, matrix products, project(): jnp.dot(flattened, weight, preferred_element_type=jnp.float32)  29.2 us
    gather x4, local copies, waits for them, and re-layouts, window_attend(): jnp.take(jnp.take(frame_cells, row_index, axis=0), col_index, axis=1)  11.8 us
    another operation x2, local copies, waits for them, and re-layouts, body(): payload[None]  11.2 us
  transfers between devices with their start and end apart: 6, of which 4 were waited for; matrix products, arithmetic and copies ran while one was open for 24% of the time, Pallas kernels for 0%

commit v1 on v0

v1 whole, which is shorter than its diff:
```python
import functools

import jax
import jax.numpy as jnp
from jax import lax
from jax.experimental import pallas as pl
from jax.experimental.pallas import tpu as pltpu
from jax.sharding import PartitionSpec as P

HEADS = 12
HEAD_DIM = 88
D = 1408
E = 1056
EP = 1152
WIN = 208
ROWS = 2 * WIN
POS = 13
TROWS = POS * 32
EPSILON = 1e-06
SCALE = HEAD_DIM ** (-0.5)
MESH = pl.DeviceIdType.MESH
F32 = jnp.float32
BF16 = jnp.bfloat16
COPIES = 72


def div(values, by):
    return lax.shift_right_logical(values * (-(-65536 // by)), 16)


def mod(values, by):
    return values - by * div(values, by)


def wrap(values, size):
    return values - jnp.where(values >= size, size, 0)


def iota(shape, axis):
    return lax.broadcasted_iota(jnp.int32, shape, axis)


def one_hot(index, columns):
    hit = index == iota((index.shape[0], columns), 1)
    return jnp.where(hit, F32(1.0), F32(0.0)).astype(BF16)


def matmul(left, right):
    return jnp.dot(left, right, preferred_element_type=F32)


def matmul_nt(left, right):
    return lax.dot_general(left, right, (((1,), (1,)), ((), ())), preferred_element_type=F32)


def tiles(width, step, do):
    whole = width // step

    def one(n, carry):
        do(pl.ds(pl.multiple_of(n * step, step), step))
        return carry

    lax.fori_loop(0, whole, one, 0)
    if width % step:
        do(pl.ds(whole * step, width % step))


def normalize(source, target, gain_ref, bias_ref, valid):
    def one(n, carry):
        rows = pl.ds(pl.multiple_of(n * 32, 32), 32)
        widened = source[rows, :].astype(F32)
        average = jnp.mean(widened, axis=-1, keepdims=True)
        centered = widened - average
        variance = jnp.mean(centered * centered, axis=-1, keepdims=True)
        normed = centered * lax.rsqrt(variance + EPSILON) * gain_ref[...] + bias_ref[...]
        keep = valid(n * 32 + iota((32, 1), 0))
        target[rows, :] = jnp.where(keep, normed, F32(0.0)).astype(BF16)
        return carry

    lax.fori_loop(0, ROWS // 32, one, 0)


def project(normed, full, qkv):
    def one(kind, carry):
        def tile(columns):
            qkv[kind, :, columns] = matmul(normed[...], full[kind, :, columns]).astype(BF16)

        tiles(EP, 256, tile)
        return carry

    lax.fori_loop(0, 3, one, 0)


def attend(qkv, mix, rows, allowed):
    count = allowed.shape[0]
    for head in range(HEADS):
        low = HEAD_DIM * head
        first = low // 128 * 128
        last = -(-(low + HEAD_DIM) // 128) * 128
        lane = first + iota((count, last - first), 1)
        own = (lane >= low) & (lane < low + HEAD_DIM)
        zero = jnp.zeros((count, last - first), BF16)
        query = qkv[0, rows, first:last]
        keys = jnp.where(own, qkv[1, rows, first:last], zero)
        values = jnp.where(own, qkv[2, rows, first:last], zero)
        weights = jnp.where(allowed, jnp.exp(matmul_nt(query, keys) * SCALE), F32(0.0))
        total = jnp.sum(weights, axis=-1, keepdims=True)
        shares = (weights * (1.0 / total)).astype(BF16)
        mixed = matmul(shares, values).astype(BF16)
        if low % 128 == 0:
            mix[rows, first:last] = mixed
        else:
            mix[rows, first : first + 128] = mix[rows, first : first + 128] + mixed[:, :128]
            if last - first > 128:
                mix[rows, first + 128 : last] = mixed[:, 128:]


def out_project(mix, full, residual, store):
    def tile(columns):
        product = matmul_nt(mix[...], full[3, columns, :])
        store(columns, (residual[:, columns].astype(F32) + product).astype(BF16))

    tiles(D, 256, tile)


def gather_steps(place, shard, zbuf, full, z_send, z_recv, z_local, send_sem, recv_sem, pending):
    y, zh, x, zl, c = place
    dev = device
    core_of = lax.div(zh, 2)
    is_sender = core_of == c
    mine = lax.rem(zh, 2)

    def z_copy(step):
        return pltpu.make_async_remote_copy(
            src_ref=shard.at[x],
            dst_ref=zbuf.at[mine],
            send_sem=z_send.at[step - 1],
            recv_sem=z_recv.at[mine],
            device_id=dev(y, lax.rem(zh + step, 4), x, zl, c),
            device_id_type=MESH,
        )

    def z_own():
        return pltpu.make_async_copy(shard.at[x], zbuf.at[mine], z_local)

    @pl.when(is_sender)
    def _():
        for step in (1, 3, 2):
            z_copy(step).start()
        z_own().start()

    def z_finish():
        @pl.when(is_sender)
        def _():
            for step in (1, 3, 2):
                z_copy(step).wait_send()

    pending.append(z_finish)
    yield

    for k in range(2):
        @pl.when(zh != 2 * c + k)
        def _():
            pltpu.make_async_remote_copy(
                src_ref=shard.at[x],
                dst_ref=zbuf.at[k],
                send_sem=z_send.at[0],
                recv_sem=z_recv.at[k],
                device_id=dev(y, zh, x, zl, 1 - c),
                device_id_type=MESH,
            ).wait_recv()

    @pl.when(is_sender)
    def _():
        z_own().wait()

    def region(kind, row, core, low, count):
        start = pl.multiple_of(352 * lax.rem(y + row + 4, 4) + 176 * core + low, 16)
        return full.at[lax.rem(x + kind + 4, 4), pl.ds(start, count), :]

    base = pl.multiple_of(352 * y + 176 * c, 16)
    both = jnp.concatenate([zbuf[0].astype(F32), zbuf[1].astype(F32)], axis=0)
    full[x, pl.ds(base, 176), :] = both.astype(BF16)

    xp, xm = dev(y, zh, lax.rem(x + 1, 4), zl, c), dev(y, zh, lax.rem(x + 3, 4), zl, c)
    yp, ym = dev(lax.rem(y + 1, 4), zh, x, zl, c), dev(lax.rem(y + 3, 4), zh, x, zl, c)
    sibling = dev(y, zh, x, zl, 1 - c)
    counter = [0]

    def copy(k, piece, target):
        return pltpu.make_async_remote_copy(
            src_ref=piece,
            dst_ref=piece,
            send_sem=send_sem.at[k],
            recv_sem=recv_sem.at[k],
            device_id=target,
            device_id_type=MESH,
        )

    def send(piece, target):
        k = counter[0]
        counter[0] += 1
        made = copy(k, piece, target)
        made.start()
        pending.append(made.wait_send)
        return k

    def recv(k, piece):
        copy(k, piece, sibling).wait_recv()

    def part_a(kind, row, low=0, count=96, core=c):
        return region(kind, row, core, low, count)

    def part_b(kind, row, low=0, count=80, core=c):
        return region(kind, row, core, 96 + low, count)

    arriving = []

    def share(part, kind, row):
        arriving.append((send(part(kind, row), sibling), part(kind, row, core=1 - c)))

    class Ring:
        def __init__(self, part, along_x, at, plus, minus, halves):
            self.part, self.along_x, self.at = part, along_x, at
            self.plus, self.minus, self.halves = plus, minus, halves
            own = self.piece(0)
            self.k_plus = send(own, plus)
            self.k_minus = send(own, minus)

        def spot(self, step):
            return (step, self.at) if self.along_x else (self.at, step)

        def piece(self, step, *cut):
            return self.part(*self.spot(step), *cut)

        def near(self):
            low, high = self.halves
            recv(self.k_plus, self.piece(-1))
            self.f_plus = send(self.piece(-1, 0, low), self.plus)
            recv(self.k_minus, self.piece(1))
            self.f_minus = send(self.piece(1, low, high), self.minus)

        def far(self):
            low, high = self.halves
            recv(self.f_plus, self.piece(2, 0, low))
            recv(self.f_minus, self.piece(2, low, high))

    def ring_a1():
        return Ring(part_a, True, 0, xp, xm, (48, 48))

    def ring_b1():
        return Ring(part_b, False, 0, yp, ym, (48, 32))

    def ring_a2(kind):
        return Ring(part_a, False, kind, yp, ym, (48, 48))

    def ring_b2(row):
        return Ring(part_b, True, row, xp, xm, (48, 32))

    a1, b1 = ring_a1(), ring_b1()
    seconds = [ring_a2(0), ring_b2(0)]
    share(part_a, 0, 0)
    share(part_b, 0, 0)
    yield
    a1.near()
    b1.near()
    for step in (-1, 1):
        seconds += [ring_a2(step), ring_b2(step)]
    for step in (-1, 1):
        share(part_a, step, 0)
        share(part_b, 0, step)
    yield
    a1.far()
    b1.far()
    seconds += [ring_a2(2), ring_b2(2)]
    share(part_a, 2, 0)
    share(part_b, 0, 2)
    for ring in seconds[:4]:
        ring.near()
        for step in (-1, 1):
            share(ring.part, *ring.spot(step))
    yield
    for ring in seconds[4:]:
        ring.near()
        for step in (-1, 1):
            share(ring.part, *ring.spot(step))
    for ring in seconds[:4]:
        ring.far()
        share(ring.part, *ring.spot(2))
    yield
    for ring in seconds[4:]:
        ring.far()
        share(ring.part, *ring.spot(2))
    for k, piece in arriving:
        recv(k, piece)
    assert counter[0] == COPIES, counter
    yield


def device(y, zh, x, zl, c):
    return (y * 4 + zh, x * 4 + zl * 2 + c)


def advance(steps):
    next(steps, None)


def kernel(
    slots, shifts, tokens, shard1, shard2, gain1, bias1, gain2, bias2, out,
    full1, full2, zbuf1, zbuf2, frames, p_in, p_out, xw, xn, qkv, mix, mid2, snd, rbuf, ret, obuf,
    z_send, z_recv, z_local, g_send, g_recv, e1_send, e1_recv, e1_local, m_sem,
    e2_send, e2_recv, e2_local, e3_send, e3_recv, e3_local,
):
    tm, space = lax.axis_index("tm"), lax.axis_index("space")
    y, zh = lax.div(tm, 4), lax.rem(tm, 4)
    x, zl, c = lax.div(space, 4), lax.rem(lax.div(space, 2), 2), lax.rem(space, 2)
    place = (y, zh, x, zl, c)
    sibling = device(y, zh, x, zl, 1 - c)
    video_t = lax.rem(zh - y + 4, 4)
    is_self = video_t == x
    pending = []

    barrier = pltpu.get_barrier_semaphore()

    def greet(target):
        pl.semaphore_signal(barrier, inc=1, device_id=target, device_id_type=MESH)

    greet(sibling)
    for step in range(1, 8):
        greet(device(y, zh, lax.rem(x + step // 2, 4), lax.rem(zl + step % 2, 2), c))

    def greet_times(n, carry):
        other = lax.rem(tm + n, 16)
        greet((other, space))
        return carry

    lax.fori_loop(1, 16, greet_times, 0)

    def greet_sources(n, carry):
        other = lax.rem(tm + lax.div(n, 2), 16)
        zl_other = lax.rem(zl + lax.rem(n, 2), 2)

        @pl.when(jnp.logical_not(is_self & (n == 0)))
        def _():
            greet((other, video_t * 4 + zl_other * 2 + c))

        return carry

    lax.fori_loop(0, 32, greet_sources, 0)
    pl.semaphore_wait(barrier, 55 - jnp.where(is_self, 1, 0))

    g1 = gather_steps(
        place, shard1, zbuf1, full1, z_send.at[0], z_recv.at[0], z_local.at[0],
        g_send.at[0], g_recv.at[0], pending,
    )
    g2 = gather_steps(
        place, shard2, zbuf2, full2, z_send.at[1], z_recv.at[1], z_local.at[1],
        g_send.at[1], g_recv.at[1], pending,
    )
    advance(g1)

    own_tile = pltpu.make_async_copy(tokens.at[zl * 4 + x], frames.at[space], e1_local)
    own_tile.start()
    for n, step in enumerate((2, 6, 1, 3, 7, 4, 5)):
        xo, zo = lax.rem(x + step // 2, 4), lax.rem(zl + step % 2, 2)
        made = pltpu.make_async_remote_copy(
            src_ref=tokens.at[zo * 4 + xo],
            dst_ref=frames.at[space],
            send_sem=e1_send.at[n],
            recv_sem=e1_recv.at[space],
            device_id=device(y, zh, xo, zo, c),
            device_id_type=MESH,
        )
        made.start()
        pending.append(made.wait_send)

    shift_r, shift_c = shifts[x, 0], shifts[x, 1]

    row = iota((ROWS, 1), 0)
    wc = div(row, WIN)
    spot = row - wc * WIN
    pr = div(spot, 14)
    pc = spot - 14 * pr
    r = wrap(14 * c + pr + shift_r, 28)
    col = wrap(14 * wc + pc + shift_c, 28)
    tile = 4 * div(r, 7) + div(col, 7)
    slot = jnp.zeros_like(tile)
    for s in range(16):
        slot = jnp.where(tile == slots[s], s, slot)
    index = slot * 64 + mod(r, 7) * 7 + mod(col, 7)
    p_in[...] = one_hot(jnp.where(spot < 196, index, -1), 1024)

    advance(g1)

    row = iota((512, 1), 0)
    slot8 = div(row, 64)
    p = mod(row, 16)
    j = POS * mod(div(row, 16), 4) + p
    tile = jnp.zeros_like(row)
    for n in range(8):
        tile = jnp.where(slot8 == n, slots[4 * (n // 2) + 2 * (n % 2) + c], tile)
    jr = div(j, 7)
    r = 7 * div(tile, 4) + jr
    col = 7 * mod(tile, 4) + (j - 7 * jr)
    sr = wrap(r + 28 - shift_r, 28)
    sc = wrap(col + 28 - shift_c, 28)
    wr, wc = div(sr, 14), div(sc, 14)
    index = wr * ROWS + wc * WIN + (sr - 14 * wr) * 14 + (sc - 14 * wc)
    p_out[...] = one_hot(jnp.where((p < POS) & (j < 49), index, -1), 2 * ROWS)

    own_tile.wait()

    def tile_copy(s, n):
        return pltpu.make_async_remote_copy(
            src_ref=frames.at[s],
            dst_ref=frames.at[s],
            send_sem=e1_send.at[7 + n],
            recv_sem=e1_recv.at[s],
            device_id=sibling,
            device_id_type=MESH,
        )

    for n, step in enumerate((0, 2, 6, 1, 3, 7, 4, 5)):
        xo, zo = lax.rem(x + step // 2, 4), lax.rem(zl + step % 2, 2)
        s = xo * 4 + zo * 2 + c
        made = tile_copy(s, n)
        if step:
            made.wait_recv()
        made.start()
        pending.append(made.wait_send)
    advance(g1)
    for step in range(8):
        s = 4 * (step // 2) + 2 * (step % 2) + 1 - c
        tile_copy(s, 0).wait_recv()

    def pick(columns):
        cells = frames[:, :, columns]
        cells = cells.reshape(1024, cells.shape[2])
        xw[:, columns] = matmul(p_in[...], cells).astype(BF16)

    tiles(D, 256, pick)

    def in_window(rows):
        return rows - jnp.where(rows >= WIN, WIN, 0) < 196

    normalize(xw, xn, gain1, bias1, in_window)
    advance(g1)
    advance(g1)
    advance(g1)
    advance(g2)
    project(xn, full1, qkv)
    advance(g2)

    def regions(shape, axis, column):
        at = iota(shape, axis)
        down = div(at, 14)
        across = at - 14 * down
        kind = 2 * jnp.where(14 * c + down >= 28 - shift_r, 1, 0)
        kind = kind + jnp.where(14 * column + across >= 28 - shift_c, 1, 0)
        return jnp.where(at < 196, kind, -1)

    for column in range(2):
        allowed = regions((WIN, 1), 0, column) == regions((1, WIN), 1, column)
        attend(qkv, mix, pl.ds(column * WIN, WIN), allowed)
        advance(g2)

    def keep_middle(columns, values):
        mid2[c, :, columns] = values

    out_project(mix, full1, xw, keep_middle)

    swap = pltpu.make_async_remote_copy(
        src_ref=mid2.at[c],
        dst_ref=mid2.at[c],
        send_sem=m_sem.at[0],
        recv_sem=m_sem.at[1],
        device_id=sibling,
        device_id_type=MESH,
    )
    swap.start()
    pending.append(swap.wait_send)
    pltpu.make_async_remote_copy(
        src_ref=mid2.at[1 - c],
        dst_ref=mid2.at[1 - c],
        send_sem=m_sem.at[0],
        recv_sem=m_sem.at[1],
        device_id=sibling,
        device_id_type=MESH,
    ).wait_recv()

    def spread(columns):
        cells = mid2[:, :, columns]
        width = cells.shape[2]
        moved = matmul(p_out[...], cells.reshape(2 * ROWS, width)).astype(BF16)
        snd[:, :, columns] = moved.reshape(32, 16, width)

    tiles(D, 256, spread)

    time = 2 * tm + zl

    def row_copy(n):
        dx, dz, dq = lax.div(n, 8), lax.rem(lax.div(n, 4), 2), lax.rem(n, 4)
        xo, zo, q = lax.rem(x + dx, 4), lax.rem(zl + dz, 2), lax.rem(y + dq, 4)
        return pltpu.make_async_remote_copy(
            src_ref=snd.at[(xo * 2 + zo) * 4 + q],
            dst_ref=rbuf.at[time],
            send_sem=e2_send.at[n],
            recv_sem=e2_recv.at[time],
            device_id=device(q, lax.rem(q + x, 4), xo, zo, c),
            device_id_type=MESH,
        )

    own_rows = pltpu.make_async_copy(snd.at[(x * 2 + zl) * 4 + y], rbuf.at[time], e2_local)

    def start_rows(n, carry):
        @pl.when(jnp.logical_not(is_self & (n == 0)))
        def _():
            row_copy(n).start()

        return carry

    lax.fori_loop(0, 32, start_rows, 0)

    @pl.when(is_self)
    def _():
        own_rows.start()
        own_rows.wait()

    advance(g2)
    advance(g2)

    def wait_rows(n, carry):
        @pl.when(jnp.logical_not(is_self & (n == time)))
        def _():
            pltpu.make_async_remote_copy(
                src_ref=snd.at[0],
                dst_ref=rbuf.at[n],
                send_sem=e2_send.at[0],
                recv_sem=e2_recv.at[n],
                device_id=sibling,
                device_id_type=MESH,
            ).wait_recv()

        return carry

    lax.fori_loop(0, 32, wait_rows, 0)

    row = iota((TROWS, 1), 0)
    at = div(row, 32)
    by_position = one_hot((row - 32 * at) * 16 + at, 512)

    def turn(columns):
        cells = rbuf[:, :, columns]
        cells = cells.reshape(512, cells.shape[2])
        xw[:, columns] = matmul(by_position, cells).astype(BF16)

    tiles(D, 256, turn)
    normalize(xw, xn, gain2, bias2, lambda rows: div(rows, 32) + POS * y < 49)
    advance(g2)
    project(xn, full2, qkv)

    for first, count in ((0, 128), (128, 128), (256, 128), (384, 32)):
        left, right = iota((count, 1), 0), iota((1, count), 1)
        attend(qkv, mix, pl.ds(first, count), div(left, 32) == div(right, 32))

    def keep_encoded(columns, values):
        xn[:, columns] = values

    out_project(mix, full2, xw, keep_encoded)

    row = iota((512, 1), 0)
    at = div(row, 16)
    p = row - 16 * at
    by_time = one_hot(jnp.where(p < POS, p * 32 + at, -1), TROWS)

    def turn_back(columns):
        moved = matmul(by_time, xn[:, columns]).astype(BF16)
        ret[:, :, columns] = moved.reshape(32, 16, moved.shape[1])

    tiles(D, 256, turn_back)

    def back_copy(n):
        other = lax.rem(tm + n, 16)
        return pltpu.make_async_remote_copy(
            src_ref=ret.at[pl.ds(2 * other, 2)],
            dst_ref=obuf.at[tm],
            send_sem=e3_send.at[n],
            recv_sem=e3_recv.at[tm],
            device_id=(other, space),
            device_id_type=MESH,
        )

    def start_back(n, carry):
        back_copy(n).start()
        return carry

    lax.fori_loop(1, 16, start_back, 0)
    own_back = pltpu.make_async_copy(ret.at[pl.ds(2 * tm, 2)], obuf.at[tm], e3_local)
    own_back.start()
    own_back.wait()

    def wait_back(n, carry):
        other = lax.rem(tm + n, 16)
        pltpu.make_async_remote_copy(
            src_ref=obuf.at[other],
            dst_ref=obuf.at[other],
            send_sem=e3_send.at[0],
            recv_sem=e3_recv.at[other],
            device_id=sibling,
            device_id_type=MESH,
        ).wait_recv()
        return carry

    lax.fori_loop(1, 16, wait_back, 0)

    row = iota((64, 1), 0)
    q = div(row, POS)
    join = one_hot(jnp.where(row < 49, q * 16 + row - POS * q, -1), 64)
    for t in range(2):
        for v in range(4):
            parts = [obuf[4 * n + (n + v) % 4, t] for n in range(4)]
            whole = matmul(join, jnp.concatenate(parts, axis=0)).astype(BF16)
            out[t, v] = whole[:49]

    for finish in pending:
        finish()

    def finish_rows(n, carry):
        @pl.when(jnp.logical_not(is_self & (n == 0)))
        def _():
            row_copy(n).wait_send()

        return carry

    lax.fori_loop(0, 32, finish_rows, 0)

    def finish_back(n, carry):
        back_copy(n).wait_send()
        return carry

    lax.fori_loop(1, 16, finish_back, 0)


def stack_weights(w_qkv, w_out):
    rows = w_qkv.shape[0]
    kinds = w_qkv.reshape(rows, 3, E).transpose(1, 0, 2)
    return jnp.pad(jnp.concatenate([kinds, w_out.T[None]], axis=0), ((0, 0), (0, 0), (0, EP - E)))


def body(
    tokens, tile_of_slot, shifts, norm_gain_space, norm_bias_space, w_qkv_space, w_out_space,
    norm_gain_time, norm_bias_time, w_qkv_time, w_out_time,
):
    cells = jnp.pad(tokens.reshape(8, 49, D), ((0, 0), (0, 15), (0, 0)))
    smem = pl.BlockSpec(memory_space=pltpu.SMEM)
    vmem = pl.BlockSpec(memory_space=pltpu.VMEM)
    anywhere = pl.BlockSpec(memory_space=pl.ANY)
    dma = pltpu.SemaphoreType.DMA
    encoded = pl.pallas_call(
        kernel,
        out_shape=jax.ShapeDtypeStruct((2, 4, 49, D), BF16),
        in_specs=[smem, smem, anywhere, anywhere, anywhere, vmem, vmem, vmem, vmem],
        out_specs=vmem,
        scratch_shapes=[
            pltpu.VMEM((4, D, EP), BF16),
            pltpu.VMEM((4, D, EP), BF16),
            pltpu.VMEM((2, 88, EP), BF16),
            pltpu.VMEM((2, 88, EP), BF16),
            pltpu.VMEM((16, 64, D), BF16),
            pltpu.VMEM((ROWS, 1024), BF16),
            pltpu.VMEM((512, 2 * ROWS), BF16),
            pltpu.VMEM((ROWS, D), BF16),
            pltpu.VMEM((ROWS, D), BF16),
            pltpu.VMEM((3, ROWS, EP), BF16),
            pltpu.VMEM((ROWS, EP), BF16),
            pltpu.VMEM((2, ROWS, D), BF16),
            pltpu.VMEM((32, 16, D), BF16),
            pltpu.VMEM((32, 16, D), BF16),
            pltpu.VMEM((32, 16, D), BF16),
            pltpu.VMEM((16, 2, 16, D), BF16),
            dma((2, 3)), dma((2, 2)), dma((2,)), dma((2, COPIES)), dma((2, COPIES)),
            dma((15,)), dma((16,)), dma, dma((2,)),
            dma((32,)), dma((32,)), dma, dma((16,)), dma((16,)), dma,
        ],
        compiler_params=pltpu.CompilerParams(
            collective_id=0, has_side_effects=True, vmem_limit_bytes=60 * 1024 * 1024
        ),
        cost_estimate=pl.CostEstimate(flops=12_000_000_000, bytes_accessed=40_000_000, transcendentals=2_000_000),
    )(
        tile_of_slot, shifts, cells, stack_weights(w_qkv_space, w_out_space),
        stack_weights(w_qkv_time, w_out_time),
        norm_gain_space[None], norm_bias_space[None], norm_gain_time[None], norm_bias_time[None],
    )
    return encoded.reshape(tokens.shape)


def solution(mesh):
    placed = (
        P("tm", "space", None, None, None), P(), P(), P(), P(), P("tm", None), P(None, "tm"),
        P(), P(), P("tm", None), P(None, "tm"),
    )
    return jax.shard_map(
        body,
        mesh=mesh,
        in_specs=placed,
        out_specs=P("tm", "space", None, None, None),
        check_vma=False,
    )
```

time: 537 us -> 216 us (0.40); the launches traced: 527 us -> 215 us
  waiting for transfers between devices: 243 us -> 0 us
  Pallas kernels: 0 us -> 199 us
  blocking collectives: 105 us -> 0 us
  local copies, waits for them, and re-layouts: 99.3 us -> 14 us
  matrix products: 35 us -> 0 us
  between operations: 15.4 us -> 0.07 us
  other arithmetic: 15.1 us -> 1.34 us
  starting transfers between devices: 13.2 us -> 0 us
    pallas_call x0 -> x1, Pallas kernels: none -> 199 us  [body(): pl.pallas_call(kernel, out_shape=jax.ShapeDtypeStruct((2, 4, 49, D), BF16...]
    all_gather x4 -> x0, waiting for transfers between devices: 121 us -> none  [the longest x1 121 us: body(): lax.all_gather(w_qkv_space, 'tm', axis=0, tiled=True)]
    all_to_all x2 -> x0, waiting for transfers between devices: 120 us -> none  [the longest x1 67.2 us: body(): lax.all_to_all(grouped, 'tm', split_axis=1, concat_axis=0, tiled=True)]
    all_to_all x2 -> x0, blocking collectives: 105 us -> none  [the longest x1 61.9 us: body(): lax.all_to_all(back_slots, 'space', split_axis=0, concat_axis=1, tiled=True)]
    dot_general x8 -> x0, matrix products: 35 us -> none  [the longest x4 29.2 us: project(): jnp.dot(flattened, weight, preferred_element_type=jnp.float32)]
    gather x14 -> x0, local copies, waits for them, and re-layouts: 24.1 us -> none  [the longest x4 11.8 us: window_attend(): jnp.take(jnp.take(frame_cells, row_index, axis=0), col_index, axis=1)]
    reshape x10 -> x5, local copies, waits for them, and re-layouts: 29.2 us -> 5.29 us  [the longest x1 2.72 us: body(): return encoded.reshape(tokens.shape)]
    all_to_all x2 -> x0, starting transfers between devices: 13.1 us -> none  [the longest x1 6.71 us: body(): lax.all_to_all(grouped, 'tm', split_axis=1, concat_axis=0, tiled=True)]
  transfers between devices with their start and end apart: 6 -> 0, of which waited for: 4 -> 0; matrix products, arithmetic and copies ran while one was open for 24% -> 0% of each run, Pallas kernels for 0% -> 0%
where the time goes in v1:
time: 216 us; the launch traced here: 215 us
  Pallas kernels  199 us (92%)
  local copies, waits for them, and re-layouts  14 us (6%)
    pallas_call x1, Pallas kernels, body(): pl.pallas_call(kernel, out_shape=jax.ShapeDtypeStruct((2, 4, 49, D), BF16...  199 us

profile of v1, /device:TPU:35, one launch (start us, length us, event | category | flops | bytes accessed | tf_op | source)
XLA Modules:
  0.0 214.6 jit_solution(11659381581489578276)
XLA Ops:
  0.0 0.0 copy-start.1
  0.0 1.4 copy.18.shifts
  1.4 1.3 broadcast_in_dim.20.gain1
  2.7 1.3 broadcast_in_dim.21.bias1
  4.0 1.3 broadcast_in_dim.22.gain2
  5.3 1.3 broadcast_in_dim.23.bias2
  6.6 2.0 reshape.13
  8.6 0.1 copy.23
  8.7 0.0 copy-start.2
  8.7 0.0 copy-start.3
  8.7 0.0 copy-done.1
  8.7 0.4 reshape.14
  9.2 0.1 copy.22
  9.2 0.4 copy-done.2
  9.6 0.1 copy-done.3
  9.7 0.0 copy-start
  9.7 1.3 fusion.4
  11.1 0.2 copy-done
  11.3 0.1 copy.15
  11.4 1.3 pad.11.tokens
  12.7 199.2 %shard_map.109 = bf16[2,4,49,1408]{3,2,1,0:T(8,128)(2,1)} custom-call(s32[16]{0:T(128)} %slots.1, s32[4,2]{1,0:T(4,128)} %copy.18.shifts, bf16[8,64,1408]{2,1,0:T(8,128)(2,1)} %pad.11.tokens, bf16[4,88,1152]{2,1,0:T(8,128)(2,1)} %get-tuple-element.5.shard1, bf16[4,88,1152]{2,1,0:T(8,128)(2,1)} %get-tuple-element.6.shard2, f32[1,1408]{1,0:T(1,128)} %broadcast_in_dim.20.gain1, ...), custom_call_target="tpu_custom_call" | custom-call | flops 12000000000 | bytes 40000000 | tf_op jit(solution)/shard_map/pallas_call | solution.py:659
  211.9 2.7 %copy.19 = bf16[2,1,4,49,1408]{4,2,3,1,0:T(4,128)(2,1)} copy(bf16[2,1,4,49,1408]{4,3,2,0,1:T(8,128)(2,1)} %bitcast.17) | data formatting | bytes 2207744 | tf_op jit(solution)/shard_map/reshape | solution.py:694
Async XLA Ops:
  0.0 8.7 %copy-start.1 = (bf16[88,3168]{1,0:T(8,128)(2,1)S(1)}, bf16[88,3168]{1,0:T(8,128)(2,1)}, u32[]{:S(2)}) copy-start(bf16[88,3168]{1,0:T(8,128)(2,1)} %param.20) | copy-start | bytes 1672708
  8.7 0.9 copy-start.2
  8.7 1.0 copy-start.3
  9.7 1.6 copy-start

commit v2 on v1

v2 whole, which is shorter than its diff:
```python
import functools

import jax
import jax.numpy as jnp
from jax import lax
from jax.experimental import pallas as pl
from jax.experimental.pallas import tpu as pltpu
from jax.sharding import PartitionSpec as P

HEADS = 12
HEAD_DIM = 88
D = 1408
E = 1056
EP = 1152
WIN = 208
ROWS = 2 * WIN
POS = 13
TROWS = POS * 32
EPSILON = 1e-06
SCALE = HEAD_DIM ** (-0.5)
MESH = pl.DeviceIdType.MESH
F32 = jnp.float32
BF16 = jnp.bfloat16
COPIES = (72, 72)
PARTS = ((0, 768), (768, 640))


def div(values, by):
    return lax.shift_right_logical(values * (-(-65536 // by)), 16)


def mod(values, by):
    return values - by * div(values, by)


def wrap(values, size):
    return values - jnp.where(values >= size, size, 0)


def iota(shape, axis):
    return lax.broadcasted_iota(jnp.int32, shape, axis)


def one_hot(index, columns):
    hit = index == iota((index.shape[0], columns), 1)
    return jnp.where(hit, F32(1.0), F32(0.0)).astype(BF16)


def matmul(left, right):
    return jnp.dot(left, right, preferred_element_type=F32)


def matmul_nt(left, right):
    return lax.dot_general(left, right, (((1,), (1,)), ((), ())), preferred_element_type=F32)


def normalize(source, target, gain_ref, bias_ref, valid):
    def one(n, carry):
        rows = pl.ds(pl.multiple_of(n * 32, 32), 32)
        widened = source[rows, :].astype(F32)
        average = jnp.mean(widened, axis=-1, keepdims=True)
        centered = widened - average
        variance = jnp.mean(centered * centered, axis=-1, keepdims=True)
        normed = centered * lax.rsqrt(variance + EPSILON) * gain_ref[...] + bias_ref[...]
        keep = valid(n * 32 + iota((32, 1), 0))
        target[rows, :] = jnp.where(keep, normed, F32(0.0)).astype(BF16)
        return carry

    lax.fori_loop(0, ROWS // 32, one, 0)


def project(normed, full, qkv, kind):
    qkv[kind] = matmul(normed[...], full[kind]).astype(BF16)


def attend(qkv, mix, rows, allowed):
    count = allowed.shape[0]
    for head in range(HEADS):
        low = HEAD_DIM * head
        first = low // 128 * 128
        last = -(-(low + HEAD_DIM) // 128) * 128
        lane = first + iota((count, last - first), 1)
        own = (lane >= low) & (lane < low + HEAD_DIM)
        zero = jnp.zeros((count, last - first), BF16)
        query = qkv[0, rows, first:last]
        keys = jnp.where(own, qkv[1, rows, first:last], zero)
        values = jnp.where(own, qkv[2, rows, first:last], zero)
        weights = jnp.where(allowed, jnp.exp(matmul_nt(query, keys) * SCALE), F32(0.0))
        total = jnp.sum(weights, axis=-1, keepdims=True)
        shares = (weights * (1.0 / total)).astype(BF16)
        mixed = matmul(shares, values).astype(BF16)
        if low % 128 == 0:
            mix[rows, first:last] = mixed
        else:
            mix[rows, first : first + 128] = mix[rows, first : first + 128] + mixed[:, :128]
            if last - first > 128:
                mix[rows, first + 128 : last] = mixed[:, 128:]


def out_project(mix, full, residual, columns):
    product = matmul_nt(mix[...], full[3, columns, :])
    return (residual[:, columns].astype(F32) + product).astype(BF16)


def stage_shard(place, w_qkv, w_out, staged):
    x = place[2]
    staged[...] = jnp.zeros_like(staged)
    for kind in range(3):
        @pl.when(x == kind)
        def _():
            staged[:, :E] = w_qkv[:, E * kind : E * kind + E]

    @pl.when(x == 3)
    def _():
        eye = one_hot(iota((88, 1), 0), 88)
        staged[:, :E] = matmul_nt(eye, w_out[...]).astype(BF16)


def gather_steps(place, sizes, staged, zbuf, full, z_send, z_recv, z_local, send_sem, recv_sem, pending):
    y, zh, x, zl, c = place
    dev = device
    core_of = lax.div(zh, 2)
    is_sender = core_of == c
    mine = lax.rem(zh, 2)

    def z_copy(step):
        return pltpu.make_async_remote_copy(
            src_ref=staged,
            dst_ref=zbuf.at[mine],
            send_sem=z_send.at[step - 1],
            recv_sem=z_recv.at[mine],
            device_id=dev(y, lax.rem(zh + step, 4), x, zl, c),
            device_id_type=MESH,
        )

    def z_own():
        return pltpu.make_async_copy(staged, zbuf.at[mine], z_local)

    @pl.when(is_sender)
    def _():
        for step in (1, 3, 2):
            z_copy(step).start()
        z_own().start()

    def z_finish():
        @pl.when(is_sender)
        def _():
            for step in (1, 3, 2):
                z_copy(step).wait_send()

    pending.append(z_finish)
    yield

    for k in range(2):
        @pl.when(zh != 2 * c + k)
        def _():
            pltpu.make_async_remote_copy(
                src_ref=staged,
                dst_ref=zbuf.at[k],
                send_sem=z_send.at[0],
                recv_sem=z_recv.at[k],
                device_id=dev(y, zh, x, zl, 1 - c),
                device_id_type=MESH,
            ).wait_recv()

    @pl.when(is_sender)
    def _():
        z_own().wait()

    def region(kind, row, core, low, count):
        start = pl.multiple_of(352 * lax.rem(y + row + 4, 4) + 176 * core + low, 16)
        return full.at[lax.rem(x + kind + 4, 4), pl.ds(start, count), :]

    rows_a, rows_b, split_z = sizes
    low_a = 80 * zl if split_z else 0
    low_b = 96 - 48 * zl if split_z else rows_a
    base = pl.multiple_of(352 * y + 176 * c, 16)
    both = jnp.concatenate([zbuf[0].astype(F32), zbuf[1].astype(F32)], axis=0)
    full[x, pl.ds(base, 176), :] = both.astype(BF16)

    xp, xm = dev(y, zh, lax.rem(x + 1, 4), zl, c), dev(y, zh, lax.rem(x + 3, 4), zl, c)
    yp, ym = dev(lax.rem(y + 1, 4), zh, x, zl, c), dev(lax.rem(y + 3, 4), zh, x, zl, c)
    sibling = dev(y, zh, x, zl, 1 - c)
    counter = [0]

    def copy(k, piece, target):
        return pltpu.make_async_remote_copy(
            src_ref=piece,
            dst_ref=piece,
            send_sem=send_sem.at[k],
            recv_sem=recv_sem.at[k],
            device_id=target,
            device_id_type=MESH,
        )

    def send(piece, target):
        k = counter[0]
        counter[0] += 1
        made = copy(k, piece, target)
        made.start()
        pending.append(made.wait_send)
        return k

    def recv(k, piece):
        copy(k, piece, sibling).wait_recv()

    def part_a(kind, row, low=0, count=rows_a, core=c):
        return region(kind, row, core, low_a + low, count)

    def part_b(kind, row, low=0, count=rows_b, core=c):
        return region(kind, row, core, low_b + low, count)

    def part_z(kind, row, parity, low=0, count=48, core=c):
        return region(kind, row, core, 128 * parity + low, count)

    arriving = []
    half_b = 16 * ((rows_b // 16 + 1) // 2)

    inner = dev(y, zh, x, 1 - zl, c)
    outer = dev(y, lax.rem(zh + 2 * zl + 3, 4), x, 1 - zl, c)
    crossing = []

    def share(part, kind, row):
        arriving.append((send(part(kind, row), sibling), part(kind, row, core=1 - c)))
        if not split_z or part is not part_a:
            return
        if kind == 0 and row == 0:
            k = send(part_z(0, 0, 1 - zl), sibling)
            arriving.append((k, part_z(0, 0, 1 - zl, core=1 - c)))
        else:
            k_out = send(part_z(kind, row, zl, 0, 32), outer)
            k_in = send(part_z(kind, row, zl, 32, 16), inner)
            crossing.append((kind, row, k_out, k_in))

    def crossed(count):
        for kind, row, k_out, k_in in crossing[:count]:
            recv(k_out, part_z(kind, row, 1 - zl, 0, 32))
            recv(k_in, part_z(kind, row, 1 - zl, 32, 16))
            k = send(part_z(kind, row, 1 - zl), sibling)
            arriving.append((k, part_z(kind, row, 1 - zl, core=1 - c)))
        del crossing[:count]

    class Ring:
        def __init__(self, part, along_x, at, plus, minus, halves):
            self.part, self.along_x, self.at = part, along_x, at
            self.plus, self.minus, self.halves = plus, minus, halves
            own = self.piece(0)
            self.k_plus = send(own, plus)
            self.k_minus = send(own, minus)

        def spot(self, step):
            return (step, self.at) if self.along_x else (self.at, step)

        def piece(self, step, *cut):
            return self.part(*self.spot(step), *cut)

        def near(self):
            low, high = self.halves
            recv(self.k_plus, self.piece(-1))
            self.f_plus = send(self.piece(-1, 0, low), self.plus)
            recv(self.k_minus, self.piece(1))
            self.f_minus = send(self.piece(1, low, high), self.minus)

        def far(self):
            low, high = self.halves
            recv(self.f_plus, self.piece(2, 0, low))
            recv(self.f_minus, self.piece(2, low, high))

    def ring_a1():
        return Ring(part_a, True, 0, xp, xm, (48, rows_a - 48))

    def ring_b1():
        return Ring(part_b, False, 0, yp, ym, (half_b, rows_b - half_b))

    def ring_a2(kind):
        return Ring(part_a, False, kind, yp, ym, (48, rows_a - 48))

    def ring_b2(row):
        return Ring(part_b, True, row, xp, xm, (half_b, rows_b - half_b))

    a1, b1 = ring_a1(), ring_b1()
    seconds = [ring_a2(0), ring_b2(0)]
    share(part_a, 0, 0)
    share(part_b, 0, 0)
    yield
    a1.near()
    b1.near()
    for step in (-1, 1):
        seconds += [ring_a2(step), ring_b2(step)]
    for step in (-1, 1):
        share(part_a, step, 0)
        share(part_b, 0, step)
    yield
    a1.far()
    b1.far()
    seconds += [ring_a2(2), ring_b2(2)]
    share(part_a, 2, 0)
    share(part_b, 0, 2)
    yield
    for n in range(0, 8, 2):
        for ring in seconds[n : n + 2]:
            ring.near()
            for step in (-1, 1):
                share(ring.part, *ring.spot(step))
        yield
    for n in range(0, 8, 2):
        for ring in seconds[n : n + 2]:
            ring.far()
            share(ring.part, *ring.spot(2))
        if n < 6:
            yield
    yield
    crossed(len(crossing))
    for k, piece in arriving:
        recv(k, piece)
    assert counter[0] == send_sem.shape[0], counter
    yield


def device(y, zh, x, zl, c):
    return (y * 4 + zh, x * 4 + zl * 2 + c)


def advance(steps):
    next(steps, None)


def kernel(
    slots, shifts, tokens, w_qkv1, w_out1, w_qkv2, w_out2, gain1, bias1, gain2, bias2, out,
    full1, full2, staged1, staged2, zbuf1, zbuf2, tiles, frames, p_in, p_out, xw, xn, qkv, mix, mid2, snd, rbuf, ret, obuf,
    z_send, z_recv, z_local, g_send1, g_recv1, g_send2, g_recv2, e1_send, e1_recv, e1_local, m_send, m_recv,
    e2_send, e2_recv, e2_local, e3_send, e3_recv, e3_local,
):
    tm, space = lax.axis_index("tm"), lax.axis_index("space")
    y, zh = lax.div(tm, 4), lax.rem(tm, 4)
    x, zl, c = lax.div(space, 4), lax.rem(lax.div(space, 2), 2), lax.rem(space, 2)
    place = (y, zh, x, zl, c)
    sibling = device(y, zh, x, zl, 1 - c)
    video_t = lax.rem(zh - y + 4, 4)
    is_self = video_t == x
    pending = []

    barrier = pltpu.get_barrier_semaphore()

    def greet(target):
        pl.semaphore_signal(barrier, inc=1, device_id=target, device_id_type=MESH)

    greet(sibling)
    for step in range(1, 8):
        greet(device(y, zh, lax.rem(x + step // 2, 4), lax.rem(zl + step % 2, 2), c))

    def greet_times(n, carry):
        other = lax.rem(tm + n, 16)
        greet((other, space))
        return carry

    lax.fori_loop(1, 16, greet_times, 0)

    def greet_sources(n, carry):
        other = lax.rem(tm + lax.div(n, 2), 16)
        zl_other = lax.rem(zl + lax.rem(n, 2), 2)

        @pl.when(jnp.logical_not(is_self & (n == 0)))
        def _():
            greet((other, video_t * 4 + zl_other * 2 + c))

        return carry

    lax.fori_loop(0, 32, greet_sources, 0)
    greet(device(y, lax.rem(zh + 2 * zl + 3, 4), x, 1 - zl, c))
    stage_shard(place, w_qkv1, w_out1, staged1)
    pl.semaphore_wait(barrier, 56 - jnp.where(is_self, 1, 0))

    g1 = gather_steps(
        place, (96, 80, False), staged1, zbuf1, full1, z_send.at[0], z_recv.at[0], z_local.at[0],
        g_send1, g_recv1, pending,
    )
    g2 = gather_steps(
        place, (96, 80, False), staged2, zbuf2, full2, z_send.at[1], z_recv.at[1], z_local.at[1],
        g_send2, g_recv2, pending,
    )
    advance(g1)

    own_tile = pltpu.make_async_copy(tokens.at[zl * 4 + x], tiles.at[space], e1_local)
    own_tile.start()
    def send_tiles(steps):
        for step in steps:
            xo, zo = lax.rem(x + step // 2, 4), lax.rem(zl + step % 2, 2)
            made = pltpu.make_async_remote_copy(
                src_ref=tokens.at[zo * 4 + xo],
                dst_ref=tiles.at[space],
                send_sem=e1_send.at[step - 1],
                recv_sem=e1_recv.at[space],
                device_id=device(y, zh, xo, zo, c),
                device_id_type=MESH,
            )
            made.start()
            pending.append(made.wait_send)

    send_tiles((2, 6, 4))
    stage_shard(place, w_qkv2, w_out2, staged2)
    frames[...] = jnp.zeros_like(frames)
    shift_r, shift_c = shifts[x, 0], shifts[x, 1]

    row = iota((ROWS, 1), 0)
    wc = div(row, WIN)
    spot = row - wc * WIN
    pr = div(spot, 14)
    pc = spot - 14 * pr
    r = wrap(14 * c + pr + shift_r, 28)
    col = wrap(14 * wc + pc + shift_c, 28)
    tile = 4 * div(r, 7) + div(col, 7)
    slot = jnp.zeros_like(tile)
    for s in range(16):
        slot = jnp.where(tile == slots[s], s, slot)
    index = slot * 64 + mod(r, 7) * 7 + mod(col, 7)
    p_in[...] = one_hot(jnp.where(spot < 196, index, -1), 1024)

    advance(g1)
    send_tiles((1, 3, 7, 5))
    advance(g2)

    row = iota((512, 1), 0)
    slot8 = div(row, 64)
    p = mod(row, 16)
    j = POS * mod(div(row, 16), 4) + p
    tile = jnp.zeros_like(row)
    for n in range(8):
        tile = jnp.where(slot8 == n, slots[4 * (n // 2) + 2 * (n % 2) + c], tile)
    jr = div(j, 7)
    r = 7 * div(tile, 4) + jr
    col = 7 * mod(tile, 4) + (j - 7 * jr)
    sr = wrap(r + 28 - shift_r, 28)
    sc = wrap(col + 28 - shift_c, 28)
    wr, wc = div(sr, 14), div(sc, 14)
    index = wr * ROWS + wc * WIN + (sr - 14 * wr) * 14 + (sc - 14 * wc)
    p_out[...] = one_hot(jnp.where((p < POS) & (j < 49), index, -1), 2 * ROWS)

    advance(g1)

    own_tile.wait()

    def tile_copy(s, n):
        return pltpu.make_async_remote_copy(
            src_ref=tiles.at[s],
            dst_ref=tiles.at[s],
            send_sem=e1_send.at[7 + n],
            recv_sem=e1_recv.at[s],
            device_id=sibling,
            device_id_type=MESH,
        )

    for n, step in enumerate((0, 2, 6, 1, 3, 7, 4, 5)):
        xo, zo = lax.rem(x + step // 2, 4), lax.rem(zl + step % 2, 2)
        s = xo * 4 + zo * 2 + c
        made = tile_copy(s, n)
        if step:
            made.wait_recv()
        made.start()
        pending.append(made.wait_send)
    advance(g1)
    advance(g1)
    for step in range(8):
        s = 4 * (step // 2) + 2 * (step % 2) + 1 - c
        tile_copy(s, 0).wait_recv()

    def widen(s, carry):
        frames[s, :49, :] = tiles[s]
        return carry

    lax.fori_loop(0, 16, widen, 0)
    for first, width in PARTS:
        columns = slice(first, first + width)
        cells = frames[:, :, columns].reshape(1024, width)
        xw[:, columns] = matmul(p_in[...], cells).astype(BF16)
        advance(g1)

    def in_window(rows):
        return rows - jnp.where(rows >= WIN, WIN, 0) < 196

    normalize(xw, xn, gain1, bias1, in_window)
    for n in range(5):
        advance(g1)
    advance(g2)
    advance(g1)
    for kind in range(3):
        project(xn, full1, qkv, kind)
        if kind:
            advance(g2)

    def regions(shape, axis, column):
        at = iota(shape, axis)
        down = div(at, 14)
        across = at - 14 * down
        kind = 2 * jnp.where(14 * c + down >= 28 - shift_r, 1, 0)
        kind = kind + jnp.where(14 * column + across >= 28 - shift_c, 1, 0)
        return jnp.where(at < 196, kind, -1)

    for column in range(2):
        allowed = regions((WIN, 1), 0, column) == regions((1, WIN), 1, column)
        attend(qkv, mix, pl.ds(column * WIN, WIN), allowed)
        advance(g2)

    def swap(n, core):
        first, width = PARTS[n]
        piece = mid2.at[core, :, pl.ds(first, width)]
        return pltpu.make_async_remote_copy(
            src_ref=piece,
            dst_ref=piece,
            send_sem=m_send.at[n],
            recv_sem=m_recv.at[n],
            device_id=sibling,
            device_id_type=MESH,
        )

    for n, (first, width) in enumerate(PARTS):
        mid2[c, :, first : first + width] = out_project(mix, full1, xw, slice(first, first + width))
        swap(n, c).start()
        pending.append(swap(n, c).wait_send)
        advance(g2)

    time = 2 * tm + zl

    def row_copy(n, part):
        dx, dz, dq = lax.div(n, 8), lax.rem(lax.div(n, 4), 2), lax.rem(n, 4)
        xo, zo, q = lax.rem(x + dx, 4), lax.rem(zl + dz, 2), lax.rem(y + dq, 4)
        columns = pl.ds(*PARTS[part])
        return pltpu.make_async_remote_copy(
            src_ref=snd.at[(xo * 2 + zo) * 4 + q, :, columns],
            dst_ref=rbuf.at[time, :, columns],
            send_sem=e2_send.at[part, n],
            recv_sem=e2_recv.at[part, time],
            device_id=device(q, lax.rem(q + x, 4), xo, zo, c),
            device_id_type=MESH,
        )

    for part, (first, width) in enumerate(PARTS):
        columns = slice(first, first + width)
        swap(part, 1 - c).wait_recv()
        cells = mid2[:, :, columns].reshape(2 * ROWS, width)
        snd[:, :, columns] = matmul(p_out[...], cells).astype(BF16).reshape(32, 16, width)

        def start_rows(n, carry):
            @pl.when(jnp.logical_not(is_self & (n == 0)))
            def _():
                row_copy(n, part).start()

            return carry

        lax.fori_loop(0, 32, start_rows, 0)

    @pl.when(is_self)
    def _():
        own_rows = pltpu.make_async_copy(snd.at[(x * 2 + zl) * 4 + y], rbuf.at[time], e2_local)
        own_rows.start()
        own_rows.wait()

    for n in range(8):
        advance(g2)

    row = iota((TROWS, 1), 0)
    at = div(row, 32)
    by_position = one_hot((row - 32 * at) * 16 + at, 512)

    for part, (first, width) in enumerate(PARTS):
        columns = slice(first, first + width)

        def wait_rows(n, carry):
            @pl.when(jnp.logical_not(is_self & (n == time)))
            def _():
                piece = rbuf.at[n, :, pl.ds(first, width)]
                pltpu.make_async_remote_copy(
                    src_ref=piece,
                    dst_ref=piece,
                    send_sem=e2_send.at[part, 0],
                    recv_sem=e2_recv.at[part, n],
                    device_id=sibling,
                    device_id_type=MESH,
                ).wait_recv()

            return carry

        lax.fori_loop(0, 32, wait_rows, 0)
        cells = rbuf[:, :, columns].reshape(512, width)
        xw[:, columns] = matmul(by_position, cells).astype(BF16)

    normalize(xw, xn, gain2, bias2, lambda rows: div(rows, 32) + POS * y < 49)
    advance(g2)
    for kind in range(3):
        project(xn, full2, qkv, kind)

    for first, count in ((0, 128), (128, 128), (256, 128), (384, 32)):
        left, right = iota((count, 1), 0), iota((1, count), 1)
        attend(qkv, mix, pl.ds(first, count), div(left, 32) == div(right, 32))

    row = iota((512, 1), 0)
    at = div(row, 16)
    p = row - 16 * at
    by_time = one_hot(jnp.where(p < POS, p * 32 + at, -1), TROWS)

    def back_copy(n, part):
        other = lax.rem(tm + n, 16)
        columns = pl.ds(*PARTS[part])
        return pltpu.make_async_remote_copy(
            src_ref=ret.at[pl.ds(2 * other, 2), :, columns],
            dst_ref=obuf.at[tm, :, :, columns],
            send_sem=e3_send.at[part, n],
            recv_sem=e3_recv.at[part, tm],
            device_id=(other, space),
            device_id_type=MESH,
        )

    for part, (first, width) in enumerate(PARTS):
        columns = slice(first, first + width)
        encoded = out_project(mix, full2, xw, columns)
        ret[:, :, columns] = matmul(by_time, encoded).astype(BF16).reshape(32, 16, width)

        def start_back(n, carry):
            back_copy(n, part).start()
            return carry

        lax.fori_loop(1, 16, start_back, 0)
    own_back = pltpu.make_async_copy(ret.at[pl.ds(2 * tm, 2)], obuf.at[tm], e3_local)
    own_back.start()
    own_back.wait()

    row = iota((64, 1), 0)
    q = div(row, POS)
    join = one_hot(jnp.where(row < 49, q * 16 + row - POS * q, -1), 64)
    for part, (first, width) in enumerate(PARTS):
        columns = slice(first, first + width)

        def wait_back(n, carry):
            piece = obuf.at[lax.rem(tm + n, 16), :, :, pl.ds(first, width)]
            pltpu.make_async_remote_copy(
                src_ref=piece,
                dst_ref=piece,
                send_sem=e3_send.at[part, 0],
                recv_sem=e3_recv.at[part, lax.rem(tm + n, 16)],
                device_id=sibling,
                device_id_type=MESH,
            ).wait_recv()
            return carry

        lax.fori_loop(1, 16, wait_back, 0)
        for t in range(2):
            for v in range(4):
                parts = [obuf[4 * n + (n + v) % 4, t, :, columns] for n in range(4)]
                whole = matmul(join, jnp.concatenate(parts, axis=0)).astype(BF16)
                out[t, v, :, columns] = whole[:49]

    for finish in pending:
        finish()

    for part in range(len(PARTS)):
        def finish_rows(n, carry):
            @pl.when(jnp.logical_not(is_self & (n == 0)))
            def _():
                row_copy(n, part).wait_send()

            return carry

        lax.fori_loop(0, 32, finish_rows, 0)

        def finish_back(n, carry):
            back_copy(n, part).wait_send()
            return carry

        lax.fori_loop(1, 16, finish_back, 0)


def body(
    tokens, tile_of_slot, shifts, norm_gain_space, norm_bias_space, w_qkv_space, w_out_space,
    norm_gain_time, norm_bias_time, w_qkv_time, w_out_time,
):
    smem = pl.BlockSpec(memory_space=pltpu.SMEM)
    vmem = pl.BlockSpec(memory_space=pltpu.VMEM)
    anywhere = pl.BlockSpec(memory_space=pl.ANY)
    dma = pltpu.SemaphoreType.DMA
    encoded = pl.pallas_call(
        kernel,
        out_shape=jax.ShapeDtypeStruct((2, 4, 49, D), BF16),
        in_specs=[smem, smem, anywhere] + [vmem] * 8,
        out_specs=vmem,
        scratch_shapes=[
            pltpu.VMEM((4, D, EP), BF16),
            pltpu.VMEM((4, D, EP), BF16),
            pltpu.VMEM((88, EP), BF16),
            pltpu.VMEM((88, EP), BF16),
            pltpu.VMEM((2, 88, EP), BF16),
            pltpu.VMEM((2, 88, EP), BF16),
            pltpu.VMEM((16, 49, D), BF16),
            pltpu.VMEM((16, 64, D), BF16),
            pltpu.VMEM((ROWS, 1024), BF16),
            pltpu.VMEM((512, 2 * ROWS), BF16),
            pltpu.VMEM((ROWS, D), BF16),
            pltpu.VMEM((ROWS, D), BF16),
            pltpu.VMEM((3, ROWS, EP), BF16),
            pltpu.VMEM((ROWS, EP), BF16),
            pltpu.VMEM((2, ROWS, D), BF16),
            pltpu.VMEM((32, 16, D), BF16),
            pltpu.VMEM((32, 16, D), BF16),
            pltpu.VMEM((32, 16, D), BF16),
            pltpu.VMEM((16, 2, 16, D), BF16),
            dma((2, 3)), dma((2, 2)), dma((2,)), dma((COPIES[0],)), dma((COPIES[0],)), dma((COPIES[1],)), dma((COPIES[1],)),
            dma((15,)), dma((16,)), dma, dma((2,)), dma((2,)),
            dma((2, 32)), dma((2, 32)), dma, dma((2, 16)), dma((2, 16)), dma,
        ],
        compiler_params=pltpu.CompilerParams(
            collective_id=0, has_side_effects=True, vmem_limit_bytes=60 * 1024 * 1024
        ),
        cost_estimate=pl.CostEstimate(flops=12_000_000_000, bytes_accessed=40_000_000, transcendentals=2_000_000),
    )(
        tile_of_slot, shifts, tokens.reshape(8, 49, D), w_qkv_space, w_out_space, w_qkv_time, w_out_time,
        norm_gain_space, norm_bias_space, norm_gain_time, norm_bias_time,
    )
    return encoded.reshape(tokens.shape)


def solution(mesh):
    placed = (
        P("tm", "space", None, None, None), P(), P(), P(), P(), P("tm", None), P(None, "tm"),
        P(), P(), P("tm", None), P(None, "tm"),
    )
    return jax.shard_map(
        body,
        mesh=mesh,
        in_specs=placed,
        out_specs=P("tm", "space", None, None, None),
        check_vma=False,
    )
```

time: 216 us -> 192 us (0.89)
  Pallas kernels: 199 us -> 179 us
  local copies, waits for them, and re-layouts: 14 us -> 10.1 us
    pallas_call x1, Pallas kernels: 199 us -> 179 us  [body(): pl.pallas_call(kernel, out_shape=jax.ShapeDtypeStruct((2, 4, 49, D), BF16...]
    broadcast_in_dim x4 -> x0, local copies, waits for them, and re-layouts: 5.17 us -> none  [the longest x1 1.3 us: body(): norm_bias_time[None]]
    unnamed x10 -> x4, local copies, waits for them, and re-layouts: 2.26 us -> 7.33 us
    reshape x4 -> x0, local copies, waits for them, and re-layouts: 2.58 us -> none  [stack_weights(): kinds = w_qkv.reshape(rows, 3, E).transpose(1, 0, 2)]
where the time goes in v2:
time: 192 us; the launch traced here: 189 us
  Pallas kernels  179 us (93%)
  local copies, waits for them, and re-layouts  10.1 us (5%)
    pallas_call x1, Pallas kernels, body(): pl.pallas_call(kernel, out_shape=jax.ShapeDtypeStruct((2, 4, 49, D), BF16...  179 us
    unnamed x4, local copies, waits for them, and re-layouts  7.33 us

profile of v2, /device:TPU:35, one launch (start us, length us, event | category | flops | bytes accessed | tf_op | source)
XLA Modules:
  0.0 189.3 jit_solution(16841505325886721813)
XLA Ops:
  0.0 1.3 copy.13.shifts
  1.3 1.8 copy.14.w_out1
  3.1 1.8 copy.15.w_out2
  4.9 2.4 %copy.12 = bf16[2,1,4,49,1408]{4,3,2,0,1:T(8,128)(2,1)} copy(bf16[2,1,4,49,1408]{4,2,3,1,0:T(4,128)(2,1)} %param.11) | data formatting | bytes 2207744 | tf_op args[0]
  7.3 179.2 %shard_map.109 = bf16[2,4,49,1408]{3,2,1,0:T(8,128)(2,1)} custom-call(s32[16]{0:T(128)} %slots.1, s32[4,2]{1,0:T(4,128)} %copy.13.shifts, bf16[8,49,1408]{2,1,0:T(8,128)(2,1)} %bitcast.3, bf16[88,3168]{1,0:T(8,128)(2,1)} %w_qkv1.1, bf16[1056,88]{1,0:T(8,128)(2,1)} %copy.14.w_out1, bf16[88,3168]{1,0:T(8,128)(2,1)} %w_qkv2.1, bf16[1056,88]{1,0:T(8,128)(2,1)} %copy.15.w_out2, ...), custom_call_target="tpu_custom_call" | custom-call | flops 12000000000 | bytes 40000000 | tf_op jit(solution)/shard_map/pallas_call | solution.py:680
  186.6 2.7 %copy.16 = bf16[2,1,4,49,1408]{4,2,3,1,0:T(4,128)(2,1)} copy(bf16[2,1,4,49,1408]{4,3,2,0,1:T(8,128)(2,1)} %bitcast.2) | data formatting | bytes 2207744 | tf_op jit(solution)/shard_map/reshape | solution.py:717

commit v3 on v2

--- a/solution.py
+++ b/solution.py
@@ -14,8 +14,7 @@
 EP = 1152
 WIN = 208
 ROWS = 2 * WIN
-POS = 13
-TROWS = POS * 32
+TROWS = 512
 EPSILON = 1e-06
 SCALE = HEAD_DIM ** (-0.5)
 MESH = pl.DeviceIdType.MESH
@@ -54,7 +53,7 @@
     return lax.dot_general(left, right, (((1,), (1,)), ((), ())), preferred_element_type=F32)
 
 
-def normalize(source, target, gain_ref, bias_ref, valid):
+def normalize(source, target, gain_ref, bias_ref, count, valid):
     def one(n, carry):
         rows = pl.ds(pl.multiple_of(n * 32, 32), 32)
         widened = source[rows, :].astype(F32)
@@ -66,15 +65,16 @@
         target[rows, :] = jnp.where(keep, normed, F32(0.0)).astype(BF16)
         return carry
 
-    lax.fori_loop(0, ROWS // 32, one, 0)
-
-
-def project(normed, full, qkv, kind):
-    qkv[kind] = matmul(normed[...], full[kind]).astype(BF16)
+    lax.fori_loop(0, count // 32, one, 0)
+
+
+def project(normed, full, qkv, kind, count):
+    qkv[kind, :count, :] = matmul(normed[:count, :], full[kind]).astype(BF16)
 
 
 def attend(qkv, mix, rows, allowed):
     count = allowed.shape[0]
+    partial = None
     for head in range(HEADS):
         low = HEAD_DIM * head
         first = low // 128 * 128
@@ -88,18 +88,20 @@
         weights = jnp.where(allowed, jnp.exp(matmul_nt(query, keys) * SCALE), F32(0.0))
         total = jnp.sum(weights, axis=-1, keepdims=True)
         shares = (weights * (1.0 / total)).astype(BF16)
-        mixed = matmul(shares, values).astype(BF16)
-        if low % 128 == 0:
-            mix[rows, first:last] = mixed
-        else:
-            mix[rows, first : first + 128] = mix[rows, first : first + 128] + mixed[:, :128]
-            if last - first > 128:
-                mix[rows, first + 128 : last] = mixed[:, 128:]
-
-
-def out_project(mix, full, residual, columns):
-    product = matmul_nt(mix[...], full[3, columns, :])
-    return (residual[:, columns].astype(F32) + product).astype(BF16)
+        mixed = matmul(shares, values)
+        pieces = [mixed[:, n : n + 128] for n in range(0, last - first, 128)]
+        if partial is not None:
+            pieces[0] = pieces[0] + partial
+        partial = None
+        if head < HEADS - 1 and (low + HEAD_DIM) % 128:
+            partial = pieces.pop()
+        for n, piece in enumerate(pieces):
+            mix[rows, first + 128 * n : first + 128 * n + 128] = piece.astype(BF16)
+
+
+def out_project(mix, full, residual, columns, count):
+    product = matmul_nt(mix[:count, :], full[3, columns, :])
+    return (residual[:count, columns].astype(F32) + product).astype(BF16)
 
 
 def stage_shard(place, w_qkv, w_out, staged):
@@ -112,8 +114,7 @@
 
     @pl.when(x == 3)
     def _():
-        eye = one_hot(iota((88, 1), 0), 88)
-        staged[:, :E] = matmul_nt(eye, w_out[...]).astype(BF16)
+        staged[:, :E] = w_out[...]
 
 
 def gather_steps(place, sizes, staged, zbuf, full, z_send, z_recv, z_local, send_sem, recv_sem, pending):
@@ -172,8 +173,8 @@
         return full.at[lax.rem(x + kind + 4, 4), pl.ds(start, count), :]
 
     rows_a, rows_b, split_z = sizes
-    low_a = 80 * zl if split_z else 0
-    low_b = 96 - 48 * zl if split_z else rows_a
+    low_a = (176 - rows_a) * zl if split_z else 0
+    low_b = rows_a - (rows_a - 48) * zl if split_z else rows_a
     base = pl.multiple_of(352 * y + 176 * c, 16)
     both = jnp.concatenate([zbuf[0].astype(F32), zbuf[1].astype(F32)], axis=0)
     full[x, pl.ds(base, 176), :] = both.astype(BF16)
@@ -214,6 +215,7 @@
         return region(kind, row, core, 128 * parity + low, count)
 
     arriving = []
+    half_a = 16 * ((rows_a // 16 + 1) // 2)
     half_b = 16 * ((rows_b // 16 + 1) // 2)
 
     inner = dev(y, zh, x, 1 - zl, c)
@@ -267,13 +269,13 @@
             recv(self.f_minus, self.piece(2, low, high))
 
     def ring_a1():
-        return Ring(part_a, True, 0, xp, xm, (48, rows_a - 48))
+        return Ring(part_a, True, 0, xp, xm, (half_a, rows_a - half_a))
 
     def ring_b1():
         return Ring(part_b, False, 0, yp, ym, (half_b, rows_b - half_b))
 
     def ring_a2(kind):
-        return Ring(part_a, False, kind, yp, ym, (48, rows_a - 48))
+        return Ring(part_a, False, kind, yp, ym, (half_a, rows_a - half_a))
 
     def ring_b2(row):
         return Ring(part_b, True, row, xp, xm, (half_b, rows_b - half_b))
@@ -328,6 +330,7 @@
 def kernel(
     slots, shifts, tokens, w_qkv1, w_out1, w_qkv2, w_out2, gain1, bias1, gain2, bias2, out,
     full1, full2, staged1, staged2, zbuf1, zbuf2, tiles, frames, p_in, p_out, xw, xn, qkv, mix, mid2, snd, rbuf, ret, obuf,
+    snd_one, rbuf_one, ret_one, obuf_one, wide, by_time,
     z_send, z_recv, z_local, g_send1, g_recv1, g_send2, g_recv2, e1_send, e1_recv, e1_local, m_send, m_recv,
     e2_send, e2_recv, e2_local, e3_send, e3_recv, e3_local,
 ):
@@ -336,8 +339,10 @@
     x, zl, c = lax.div(space, 4), lax.rem(lax.div(space, 2), 2), lax.rem(space, 2)
     place = (y, zh, x, zl, c)
     sibling = device(y, zh, x, zl, 1 - c)
-    video_t = lax.rem(zh - y + 4, 4)
+    video_t = lax.rem(zh + y, 4)
     is_self = video_t == x
+    quarter = lax.rem(zh + 2 * zl + c, 4)
+    single = quarter == 3
     pending = []
 
     barrier = pltpu.get_barrier_semaphore()
@@ -399,8 +404,9 @@
 
     send_tiles((2, 6, 4))
     stage_shard(place, w_qkv2, w_out2, staged2)
+    wide[...] = jnp.zeros_like(wide)
     frames[...] = jnp.zeros_like(frames)
-    shift_r, shift_c = shifts[x, 0], shifts[x, 1]
+    shift_r, shift_c = shifts[0, x], shifts[1, x]
 
     row = iota((ROWS, 1), 0)
     wc = div(row, WIN)
@@ -420,10 +426,10 @@
     send_tiles((1, 3, 7, 5))
     advance(g2)
 
-    row = iota((512, 1), 0)
-    slot8 = div(row, 64)
-    p = mod(row, 16)
-    j = POS * mod(div(row, 16), 4) + p
+    row = iota((400, 1), 0)
+    last = row >= 384
+    slot8 = jnp.where(last, row - 384, div(row, 48))
+    j = jnp.where(last, 48, row - 48 * slot8)
     tile = jnp.zeros_like(row)
     for n in range(8):
         tile = jnp.where(slot8 == n, slots[4 * (n // 2) + 2 * (n % 2) + c], tile)
@@ -434,7 +440,7 @@
     sc = wrap(col + 28 - shift_c, 28)
     wr, wc = div(sr, 14), div(sc, 14)
     index = wr * ROWS + wc * WIN + (sr - 14 * wr) * 14 + (sc - 14 * wc)
-    p_out[...] = one_hot(jnp.where((p < POS) & (j < 49), index, -1), 2 * ROWS)
+    p_out[...] = one_hot(jnp.where(slot8 < 8, index, -1), 2 * ROWS)
 
     advance(g1)
 
@@ -472,19 +478,19 @@
     for first, width in PARTS:
         columns = slice(first, first + width)
         cells = frames[:, :, columns].reshape(1024, width)
-        xw[:, columns] = matmul(p_in[...], cells).astype(BF16)
+        xw[:ROWS, columns] = matmul(p_in[...], cells).astype(BF16)
         advance(g1)
 
     def in_window(rows):
         return rows - jnp.where(rows >= WIN, WIN, 0) < 196
 
-    normalize(xw, xn, gain1, bias1, in_window)
+    normalize(xw, xn, gain1, bias1, ROWS, in_window)
     for n in range(5):
         advance(g1)
     advance(g2)
     advance(g1)
     for kind in range(3):
-        project(xn, full1, qkv, kind)
+        project(xn, full1, qkv, kind, ROWS)
         if kind:
             advance(g2)
 
@@ -514,89 +520,148 @@
         )
 
     for n, (first, width) in enumerate(PARTS):
-        mid2[c, :, first : first + width] = out_project(mix, full1, xw, slice(first, first + width))
+        mid2[c, :, first : first + width] = out_project(mix, full1, xw, slice(first, first + width), ROWS)
         swap(n, c).start()
         pending.append(swap(n, c).wait_send)
         advance(g2)
 
     time = 2 * tm + zl
 
+    def row_target(n):
+        dx, dz, dh = lax.div(n, 8), lax.rem(lax.div(n, 4), 2), lax.rem(n, 4)
+        xo, zo, ho = lax.rem(x + dx, 4), lax.rem(zl + dz, 2), lax.rem(zh + dh, 4)
+        target = device(lax.rem(x - ho + 4, 4), ho, xo, zo, c)
+        return xo * 2 + zo, lax.rem(ho + 2 * zo + c, 4), target
+
     def row_copy(n, part):
-        dx, dz, dq = lax.div(n, 8), lax.rem(lax.div(n, 4), 2), lax.rem(n, 4)
-        xo, zo, q = lax.rem(x + dx, 4), lax.rem(zl + dz, 2), lax.rem(y + dq, 4)
+        s, q, target = row_target(n)
         columns = pl.ds(*PARTS[part])
         return pltpu.make_async_remote_copy(
-            src_ref=snd.at[(xo * 2 + zo) * 4 + q, :, columns],
+            src_ref=snd.at[s * 3 + q, :, columns],
             dst_ref=rbuf.at[time, :, columns],
             send_sem=e2_send.at[part, n],
             recv_sem=e2_recv.at[part, time],
-            device_id=device(q, lax.rem(q + x, 4), xo, zo, c),
+            device_id=target,
             device_id_type=MESH,
         )
+
+    def one_copy(n):
+        s, q, target = row_target(n)
+        return pltpu.make_async_remote_copy(
+            src_ref=snd_one.at[s],
+            dst_ref=rbuf_one.at[time],
+            send_sem=e2_send.at[1, n],
+            recv_sem=e2_recv.at[1, time],
+            device_id=target,
+            device_id_type=MESH,
+        )
+
+    def each_row(n, part, do):
+        away = jnp.logical_not(is_self & (n == 0))
+        q = row_target(n)[1]
+
+        @pl.when(away & (q < 3))
+        def _():
+            do(row_copy(n, part))
+
+        if part:
+            @pl.when(away & (q == 3))
+            def _():
+                do(one_copy(n))
 
     for part, (first, width) in enumerate(PARTS):
         columns = slice(first, first + width)
         swap(part, 1 - c).wait_recv()
         cells = mid2[:, :, columns].reshape(2 * ROWS, width)
-        snd[:, :, columns] = matmul(p_out[...], cells).astype(BF16).reshape(32, 16, width)
+        moved = matmul(p_out[...], cells)
+        snd[:, :, columns] = moved[:384].astype(BF16).reshape(24, 16, width)
+        for n in range(width // 128):
+            wide[:8, first // 128 + n, :] = moved[384:392, 128 * n : 128 * n + 128]
+        if part:
+            snd_one[...] = wide[:8].astype(BF16)
 
         def start_rows(n, carry):
-            @pl.when(jnp.logical_not(is_self & (n == 0)))
-            def _():
-                row_copy(n, part).start()
-
+            each_row(n, part, lambda made: made.start())
             return carry
 
         lax.fori_loop(0, 32, start_rows, 0)
 
-    @pl.when(is_self)
+    @pl.when(is_self & jnp.logical_not(single))
     def _():
-        own_rows = pltpu.make_async_copy(snd.at[(x * 2 + zl) * 4 + y], rbuf.at[time], e2_local)
+        own_rows = pltpu.make_async_copy(snd.at[(x * 2 + zl) * 3 + quarter], rbuf.at[time], e2_local)
         own_rows.start()
         own_rows.wait()
 
+    @pl.when(is_self & single)
+    def _():
+        own_rows = pltpu.make_async_copy(snd_one.at[x * 2 + zl], rbuf_one.at[time], e2_local)
+        own_rows.start()
+        own_rows.wait()
+
     for n in range(8):
         advance(g2)
 
     row = iota((TROWS, 1), 0)
     at = div(row, 32)
-    by_position = one_hot((row - 32 * at) * 16 + at, 512)
-
-    for part, (first, width) in enumerate(PARTS):
-        columns = slice(first, first + width)
-
-        def wait_rows(n, carry):
+    by_position = one_hot((row - 32 * at) * 16 + at, TROWS)
+
+    at = div(row, 16)
+    p = row - 16 * at
+    by_time[...] = one_hot(p * 32 + at, TROWS)
+
+    def wait_landed(piece, part, n):
+        pltpu.make_async_remote_copy(
+            src_ref=piece,
+            dst_ref=piece,
+            send_sem=e2_send.at[part, 0],
+            recv_sem=e2_recv.at[part, n],
+            device_id=sibling,
+            device_id_type=MESH,
+        ).wait_recv()
+
+    @pl.when(jnp.logical_not(single))
+    def _():
+        for part, (first, width) in enumerate(PARTS):
+            columns = slice(first, first + width)
+
+            def wait_rows(n, carry):
+                @pl.when(jnp.logical_not(is_self & (n == time)))
+                def _():
+                    wait_landed(rbuf.at[n, :, pl.ds(first, width)], part, n)
+
+                return carry
+
+            lax.fori_loop(0, 32, wait_rows, 0)
+            cells = rbuf[:, :, columns].reshape(TROWS, width)
+            xw[:, columns] = matmul(by_position, cells).astype(BF16)
+
+    @pl.when(single)
+    def _():
+        def wait_ones(n, carry):
             @pl.when(jnp.logical_not(is_self & (n == time)))
             def _():
-                piece = rbuf.at[n, :, pl.ds(first, width)]
-                pltpu.make_async_remote_copy(
-                    src_ref=piece,
-                    dst_ref=piece,
-                    send_sem=e2_send.at[part, 0],
-                    recv_sem=e2_recv.at[part, n],
-                    device_id=sibling,
-                    device_id_type=MESH,
-                ).wait_recv()
+                wait_landed(rbuf_one.at[n], 1, n)
 
             return carry
 
-        lax.fori_loop(0, 32, wait_rows, 0)
-        cells = rbuf[:, :, columns].reshape(512, width)
-        xw[:, columns] = matmul(by_position, cells).astype(BF16)
-
-    normalize(xw, xn, gain2, bias2, lambda rows: div(rows, 32) + POS * y < 49)
+        lax.fori_loop(0, 32, wait_ones, 0)
+        xw[...] = jnp.zeros_like(xw)
+        wide[...] = rbuf_one[...].astype(F32)
+        for n in range(11):
+            xw[:32, 128 * n : 128 * n + 128] = wide[:, n, :].astype(BF16)
+
+    normalize(xw, xn, gain2, bias2, TROWS, lambda rows: jnp.logical_not(single) | (rows < 32))
     advance(g2)
     for kind in range(3):
-        project(xn, full2, qkv, kind)
-
-    for first, count in ((0, 128), (128, 128), (256, 128), (384, 32)):
-        left, right = iota((count, 1), 0), iota((1, count), 1)
-        attend(qkv, mix, pl.ds(first, count), div(left, 32) == div(right, 32))
-
-    row = iota((512, 1), 0)
-    at = div(row, 16)
-    p = row - 16 * at
-    by_time = one_hot(jnp.where(p < POS, p * 32 + at, -1), TROWS)
+        project(xn, full2, qkv, kind, TROWS)
+
+    def attend_group(n, carry):
+        left, right = iota((128, 1), 0), iota((1, 128), 1)
+        rows = pl.ds(pl.multiple_of(n * 128, 128), 128)
+        attend(qkv, mix, rows, div(left, 32) == div(right, 32))
+        return carry
+
+    lax.fori_loop(0, 4, attend_group, 0)
 
     def back_copy(n, part):
         other = lax.rem(tm + n, 16)
@@ -610,63 +675,111 @@
             device_id_type=MESH,
         )
 
+    def back_one(n):
+        other = lax.rem(tm + n, 16)
+        return pltpu.make_async_remote_copy(
+            src_ref=ret_one.at[pl.ds(2 * other, 2)],
+            dst_ref=obuf_one.at[tm],
+            send_sem=e3_send.at[1, n],
+            recv_sem=e3_recv.at[1, tm],
+            device_id=(other, space),
+            device_id_type=MESH,
+        )
+
+    def all_back(part, do):
+        @pl.when(jnp.logical_not(single))
+        def _():
+            def one(n, carry):
+                do(back_copy(n, part))
+                return carry
+
+            lax.fori_loop(1, 16, one, 0)
+
+        if part:
+            @pl.when(single)
+            def _():
+                def one(n, carry):
+                    do(back_one(n))
+                    return carry
+
+                lax.fori_loop(1, 16, one, 0)
+
     for part, (first, width) in enumerate(PARTS):
         columns = slice(first, first + width)
-        encoded = out_project(mix, full2, xw, columns)
-        ret[:, :, columns] = matmul(by_time, encoded).astype(BF16).reshape(32, 16, width)
-
-        def start_back(n, carry):
-            back_copy(n, part).start()
+        encoded = out_project(mix, full2, xw, columns, TROWS)
+        ret[:, :, columns] = matmul(by_time[...], encoded).astype(BF16).reshape(32, 16, width)
+        for n in range(width // 128):
+            wide[:, first // 128 + n, :] = encoded[:32, 128 * n : 128 * n + 128].astype(F32)
+        if part:
+            ret_one[...] = wide[...].astype(BF16)
+        all_back(part, lambda made: made.start())
+
+    @pl.when(jnp.logical_not(single))
+    def _():
+        own_back = pltpu.make_async_copy(ret.at[pl.ds(2 * tm, 2)], obuf.at[tm], e3_local)
+        own_back.start()
+        own_back.wait()
+
+    @pl.when(single)
+    def _():
+        own_back = pltpu.make_async_copy(ret_one.at[pl.ds(2 * tm, 2)], obuf_one.at[tm], e3_local)
+        own_back.start()
+        own_back.wait()
+
+    for finish in pending:
+        finish()
+
+    for part in range(len(PARTS)):
+        def finish_rows(n, carry):
+            each_row(n, part, lambda made: made.wait_send())
             return carry
 
-        lax.fori_loop(1, 16, start_back, 0)
-    own_back = pltpu.make_async_copy(ret.at[pl.ds(2 * tm, 2)], obuf.at[tm], e3_local)
-    own_back.start()
-    own_back.wait()
-
-    row = iota((64, 1), 0)
-    q = div(row, POS)
-    join = one_hot(jnp.where(row < 49, q * 16 + row - POS * q, -1), 64)
+        lax.fori_loop(0, 32, finish_rows, 0)
+
+    def wait_back(piece, part, n):
+        pltpu.make_async_remote_copy(
+            src_ref=piece,
+            dst_ref=piece,
+            send_sem=e3_send.at[part, 0],
+            recv_sem=e3_recv.at[part, n],
+            device_id=sibling,
+            device_id_type=MESH,
+        ).wait_recv()
+
     for part, (first, width) in enumerate(PARTS):
         columns = slice(first, first + width)
 
-        def wait_back(n, carry):
-            piece = obuf.at[lax.rem(tm + n, 16), :, :, pl.ds(first, width)]
-            pltpu.make_async_remote_copy(
-                src_ref=piece,
-                dst_ref=piece,
-                send_sem=e3_send.at[part, 0],
-                recv_sem=e3_recv.at[part, lax.rem(tm + n, 16)],
-                device_id=sibling,
-                device_id_type=MESH,
-            ).wait_recv()
+        def land(n, carry):
+            q = lax.rem(lax.rem(n, 4) + 2 * zl + c, 4)
+
+            @pl.when((n != tm) & (q < 3))
+            def _():
+                wait_back(obuf.at[n, :, :, pl.ds(first, width)], part, n)
+
+            if part:
+                @pl.when((n != tm) & (q == 3))
+                def _():
+                    wait_back(obuf_one.at[n], part, n)
+
             return carry
 
-        lax.fori_loop(1, 16, wait_back, 0)
+        lax.fori_loop(0, 16, land, 0)
+        for q in range(3):
+            for v in range(4):
+                ho = lax.rem(q + 8 - 2 * zl - c, 4)
+                n = lax.rem(v - ho + 4, 4) * 4 + ho
+                for t in range(2):
+                    out[t, v, 16 * q : 16 * q + 16, columns] = obuf[n, t, :, columns]
+    for v in range(4):
+        ho = lax.rem(11 - 2 * zl - c, 4)
+        n = lax.rem(v - ho + 4, 4) * 4 + ho
         for t in range(2):
-            for v in range(4):
-                parts = [obuf[4 * n + (n + v) % 4, t, :, columns] for n in range(4)]
-                whole = matmul(join, jnp.concatenate(parts, axis=0)).astype(BF16)
-                out[t, v, :, columns] = whole[:49]
-
-    for finish in pending:
-        finish()
+            last = obuf_one[n, t].astype(F32)
+            for k in range(11):
+                out[t, v, 48:49, 128 * k : 128 * k + 128] = last[k : k + 1, :].astype(BF16)
 
     for part in range(len(PARTS)):
-        def finish_rows(n, carry):
-            @pl.when(jnp.logical_not(is_self & (n == 0)))
-            def _():
-                row_copy(n, part).wait_send()
-
-            return carry
-
-        lax.fori_loop(0, 32, finish_rows, 0)
-
-        def finish_back(n, carry):
-            back_copy(n, part).wait_send()
-            return carry
-
-        lax.fori_loop(1, 16, finish_back, 0)
+        all_back(part, lambda made: made.wait_send())
 
 
 def body(
@@ -692,16 +805,22 @@
             pltpu.VMEM((16, 49, D), BF16),
             pltpu.VMEM((16, 64, D), BF16),
             pltpu.VMEM((ROWS, 1024), BF16),
-            pltpu.VMEM((512, 2 * ROWS), BF16),
-            pltpu.VMEM((ROWS, D), BF16),
-            pltpu.VMEM((ROWS, D), BF16),
-            pltpu.VMEM((3, ROWS, EP), BF16),
-            pltpu.VMEM((ROWS, EP), BF16),
+            pltpu.VMEM((400, 2 * ROWS), BF16),
+            pltpu.VMEM((TROWS, D), BF16),
+            pltpu.VMEM((TROWS, D), BF16),
+            pltpu.VMEM((3, TROWS, EP), BF16),
+            pltpu.VMEM((TROWS, EP), BF16),
             pltpu.VMEM((2, ROWS, D), BF16),
-            pltpu.VMEM((32, 16, D), BF16),
+            pltpu.VMEM((24, 16, D), BF16),
             pltpu.VMEM((32, 16, D), BF16),
             pltpu.VMEM((32, 16, D), BF16),
             pltpu.VMEM((16, 2, 16, D), BF16),
+            pltpu.VMEM((8, 16, 128), BF16),
+            pltpu.VMEM((32, 16, 128), BF16),
+            pltpu.VMEM((32, 16, 128), BF16),
+            pltpu.VMEM((16, 2, 16, 128), BF16),
+            pltpu.VMEM((32, 16, 128), F32),
+            pltpu.VMEM((TROWS, TROWS), BF16),
             dma((2, 3)), dma((2, 2)), dma((2,)), dma((COPIES[0],)), dma((COPIES[0],)), dma((COPIES[1],)), dma((COPIES[1],)),
             dma((15,)), dma((16,)), dma, dma((2,)), dma((2,)),
             dma((2, 32)), dma((2, 32)), dma, dma((2, 16)), dma((2, 16)), dma,
@@ -711,7 +830,7 @@
         ),
         cost_estimate=pl.CostEstimate(flops=12_000_000_000, bytes_accessed=40_000_000, transcendentals=2_000_000),
     )(
-        tile_of_slot, shifts, tokens.reshape(8, 49, D), w_qkv_space, w_out_space, w_qkv_time, w_out_time,
+        tile_of_slot, shifts.T, tokens.reshape(8, 49, D), w_qkv_space, w_out_space.T, w_qkv_time, w_out_time.T,
         norm_gain_space, norm_bias_space, norm_gain_time, norm_bias_time,
     )
     return encoded.reshape(tokens.shape)

time: 192 us -> 182 us (0.948); the launches traced: 189 us -> 182 us
  local copies, waits for them, and re-layouts: 10.1 us -> 5.13 us
  Pallas kernels: 179 us -> 177 us
    unnamed x4 -> x1, local copies, waits for them, and re-layouts: 7.33 us -> 2.41 us
    pallas_call x1, Pallas kernels: 179 us -> 177 us  [body(): pl.pallas_call(kernel, out_shape=jax.ShapeDtypeStruct((2, 4, 49, D), BF16...]
where the time goes in v3:
time: 182 us
  Pallas kernels  177 us (97%)
  local copies, waits for them, and re-layouts  5.13 us (3%)
    pallas_call x1, Pallas kernels, body(): pl.pallas_call(kernel, out_shape=jax.ShapeDtypeStruct((2, 4, 49, D), BF16...  177 us

profile of v3, /device:TPU:35, one launch (start us, length us, event | category | flops | bytes accessed | tf_op | source)
XLA Modules:
  0.0 181.7 jit_solution(13554948937765348462)
XLA Ops:
  0.0 2.4 %copy.12 = bf16[2,1,4,49,1408]{4,3,2,0,1:T(8,128)(2,1)} copy(bf16[2,1,4,49,1408]{4,2,3,1,0:T(4,128)(2,1)} %param.11) | data formatting | bytes 2207744 | tf_op args[0]
  2.4 176.5 %shard_map.109 = bf16[2,4,49,1408]{3,2,1,0:T(8,128)(2,1)} custom-call(s32[16]{0:T(128)} %slots.1, s32[2,4]{1,0:T(2,128)} %bitcast.9, bf16[8,49,1408]{2,1,0:T(8,128)(2,1)} %bitcast.6, bf16[88,3168]{1,0:T(8,128)(2,1)} %w_qkv1.1, bf16[88,1056]{1,0:T(8,128)(2,1)} %bitcast.7, bf16[88,3168]{1,0:T(8,128)(2,1)} %w_qkv2.1, bf16[88,1056]{1,0:T(8,128)(2,1)} %bitcast.8, ...), custom_call_target="tpu_custom_call" | custom-call | flops 12000000000 | bytes 40000000 | tf_op jit(solution)/shard_map/pallas_call | solution.py:793
  178.9 2.7 %copy.13 = bf16[2,1,4,49,1408]{4,2,3,1,0:T(4,128)(2,1)} copy(bf16[2,1,4,49,1408]{4,3,2,0,1:T(8,128)(2,1)} %bitcast.5) | data formatting | bytes 2207744 | tf_op jit(solution)/shard_map/reshape | solution.py:836

commit v4 on v3

--- a/solution.py
+++ b/solution.py
@@ -68,8 +68,8 @@
     lax.fori_loop(0, count // 32, one, 0)
 
 
-def project(normed, full, qkv, kind, count):
-    qkv[kind, :count, :] = matmul(normed[:count, :], full[kind]).astype(BF16)
+def project(normed, full, qkv, kind, rows):
+    qkv[kind, rows, :] = matmul(normed[rows, :], full[kind]).astype(BF16)
 
 
 def attend(qkv, mix, rows, allowed):
@@ -99,9 +99,9 @@
             mix[rows, first + 128 * n : first + 128 * n + 128] = piece.astype(BF16)
 
 
-def out_project(mix, full, residual, columns, count):
-    product = matmul_nt(mix[:count, :], full[3, columns, :])
-    return (residual[:count, columns].astype(F32) + product).astype(BF16)
+def out_project(mix, full, residual, columns, rows):
+    product = matmul_nt(mix[rows, :], full[3, columns, :])
+    return (residual[rows, columns].astype(F32) + product).astype(BF16)
 
 
 def stage_shard(place, w_qkv, w_out, staged):
@@ -490,7 +490,7 @@
     advance(g2)
     advance(g1)
     for kind in range(3):
-        project(xn, full1, qkv, kind, ROWS)
+        project(xn, full1, qkv, kind, slice(0, ROWS))
         if kind:
             advance(g2)
 
@@ -520,7 +520,7 @@
         )
 
     for n, (first, width) in enumerate(PARTS):
-        mid2[c, :, first : first + width] = out_project(mix, full1, xw, slice(first, first + width), ROWS)
+        mid2[c, :, first : first + width] = out_project(mix, full1, xw, slice(first, first + width), slice(0, ROWS))
         swap(n, c).start()
         pending.append(swap(n, c).wait_send)
         advance(g2)
@@ -605,9 +605,9 @@
     at = div(row, 32)
     by_position = one_hot((row - 32 * at) * 16 + at, TROWS)
 
-    at = div(row, 16)
-    p = row - 16 * at
-    by_time[...] = one_hot(p * 32 + at, TROWS)
+    row = iota((256, 1), 0)
+    at = div(row, 8)
+    by_time[...] = one_hot((row - 8 * at) * 32 + at, 256)
 
     def wait_landed(piece, part, n):
         pltpu.make_async_remote_copy(
@@ -652,25 +652,13 @@
 
     normalize(xw, xn, gain2, bias2, TROWS, lambda rows: jnp.logical_not(single) | (rows < 32))
     advance(g2)
-    for kind in range(3):
-        project(xn, full2, qkv, kind, TROWS)
-
-    def attend_group(n, carry):
-        left, right = iota((128, 1), 0), iota((1, 128), 1)
-        rows = pl.ds(pl.multiple_of(n * 128, 128), 128)
-        attend(qkv, mix, rows, div(left, 32) == div(right, 32))
-        return carry
-
-    lax.fori_loop(0, 4, attend_group, 0)
-
-    def back_copy(n, part):
+    def back_copy(n, half):
         other = lax.rem(tm + n, 16)
-        columns = pl.ds(*PARTS[part])
         return pltpu.make_async_remote_copy(
-            src_ref=ret.at[pl.ds(2 * other, 2), :, columns],
-            dst_ref=obuf.at[tm, :, :, columns],
-            send_sem=e3_send.at[part, n],
-            recv_sem=e3_recv.at[part, tm],
+            src_ref=ret.at[half, other],
+            dst_ref=obuf.at[tm, half],
+            send_sem=e3_send.at[half, n],
+            recv_sem=e3_recv.at[half, tm],
             device_id=(other, space),
             device_id_type=MESH,
         )
@@ -680,22 +668,22 @@
         return pltpu.make_async_remote_copy(
             src_ref=ret_one.at[pl.ds(2 * other, 2)],
             dst_ref=obuf_one.at[tm],
-            send_sem=e3_send.at[1, n],
-            recv_sem=e3_recv.at[1, tm],
+            send_sem=e3_send.at[0, n],
+            recv_sem=e3_recv.at[0, tm],
             device_id=(other, space),
             device_id_type=MESH,
         )
 
-    def all_back(part, do):
+    def all_back(half, do):
         @pl.when(jnp.logical_not(single))
         def _():
             def one(n, carry):
-                do(back_copy(n, part))
+                do(back_copy(n, half))
                 return carry
 
             lax.fori_loop(1, 16, one, 0)
 
-        if part:
+        if half == 0:
             @pl.when(single)
             def _():
                 def one(n, carry):
@@ -704,19 +692,32 @@
 
                 lax.fori_loop(1, 16, one, 0)
 
-    for part, (first, width) in enumerate(PARTS):
-        columns = slice(first, first + width)
-        encoded = out_project(mix, full2, xw, columns, TROWS)
-        ret[:, :, columns] = matmul(by_time[...], encoded).astype(BF16).reshape(32, 16, width)
-        for n in range(width // 128):
-            wide[:, first // 128 + n, :] = encoded[:32, 128 * n : 128 * n + 128].astype(F32)
-        if part:
+    for half in range(2):
+        part_rows = slice(256 * half, 256 * half + 256)
+        for kind in range(3):
+            project(xn, full2, qkv, kind, part_rows)
+
+        def attend_group(n, carry):
+            left, right = iota((128, 1), 0), iota((1, 128), 1)
+            rows = pl.ds(pl.multiple_of(n * 128, 128), 128)
+            attend(qkv, mix, rows, div(left, 32) == div(right, 32))
+            return carry
+
+        lax.fori_loop(2 * half, 2 * half + 2, attend_group, 0)
+        for first, width in PARTS:
+            columns = slice(first, first + width)
+            encoded = out_project(mix, full2, xw, columns, part_rows)
+            ret[half, :, :, columns] = matmul(by_time[...], encoded).astype(BF16).reshape(16, 16, width)
+            if half == 0:
+                for n in range(width // 128):
+                    wide[:, first // 128 + n, :] = encoded[:32, 128 * n : 128 * n + 128].astype(F32)
+        if half == 0:
             ret_one[...] = wide[...].astype(BF16)
-        all_back(part, lambda made: made.start())
+        all_back(half, lambda made: made.start())
 
     @pl.when(jnp.logical_not(single))
     def _():
-        own_back = pltpu.make_async_copy(ret.at[pl.ds(2 * tm, 2)], obuf.at[tm], e3_local)
+        own_back = pltpu.make_async_copy(ret.at[:, tm], obuf.at[tm], e3_local)
         own_back.start()
         own_back.wait()
 
@@ -746,30 +747,30 @@
             device_id_type=MESH,
         ).wait_recv()
 
-    for part, (first, width) in enumerate(PARTS):
-        columns = slice(first, first + width)
-
+    for half in range(2):
         def land(n, carry):
             q = lax.rem(lax.rem(n, 4) + 2 * zl + c, 4)
 
             @pl.when((n != tm) & (q < 3))
             def _():
-                wait_back(obuf.at[n, :, :, pl.ds(first, width)], part, n)
-
-            if part:
+                wait_back(obuf.at[n, half], half, n)
+
+            if half == 0:
                 @pl.when((n != tm) & (q == 3))
                 def _():
-                    wait_back(obuf_one.at[n], part, n)
+                    wait_back(obuf_one.at[n], half, n)
 
             return carry
 
         lax.fori_loop(0, 16, land, 0)
-        for q in range(3):
-            for v in range(4):
-                ho = lax.rem(q + 8 - 2 * zl - c, 4)
-                n = lax.rem(v - ho + 4, 4) * 4 + ho
-                for t in range(2):
-                    out[t, v, 16 * q : 16 * q + 16, columns] = obuf[n, t, :, columns]
+    for q in range(3):
+        for v in range(4):
+            ho = lax.rem(q + 8 - 2 * zl - c, 4)
+            n = lax.rem(v - ho + 4, 4) * 4 + ho
+            early, late = obuf[n, 0].astype(F32), obuf[n, 1].astype(F32)
+            for t in range(2):
+                rows = jnp.concatenate([early[8 * t : 8 * t + 8], late[8 * t : 8 * t + 8]], axis=0)
+                out[t, v, 16 * q : 16 * q + 16, :] = rows.astype(BF16)
     for v in range(4):
         ho = lax.rem(11 - 2 * zl - c, 4)
         n = lax.rem(v - ho + 4, 4) * 4 + ho
@@ -778,8 +779,8 @@
             for k in range(11):
                 out[t, v, 48:49, 128 * k : 128 * k + 128] = last[k : k + 1, :].astype(BF16)
 
-    for part in range(len(PARTS)):
-        all_back(part, lambda made: made.wait_send())
+    for half in range(2):
+        all_back(half, lambda made: made.wait_send())
 
 
 def body(
@@ -813,14 +814,14 @@
             pltpu.VMEM((2, ROWS, D), BF16),
             pltpu.VMEM((24, 16, D), BF16),
             pltpu.VMEM((32, 16, D), BF16),
-            pltpu.VMEM((32, 16, D), BF16),
+            pltpu.VMEM((2, 16, 16, D), BF16),
             pltpu.VMEM((16, 2, 16, D), BF16),
             pltpu.VMEM((8, 16, 128), BF16),
             pltpu.VMEM((32, 16, 128), BF16),
             pltpu.VMEM((32, 16, 128), BF16),
             pltpu.VMEM((16, 2, 16, 128), BF16),
             pltpu.VMEM((32, 16, 128), F32),
-            pltpu.VMEM((TROWS, TROWS), BF16),
+            pltpu.VMEM((256, 256), BF16),
             dma((2, 3)), dma((2, 2)), dma((2,)), dma((COPIES[0],)), dma((COPIES[0],)), dma((COPIES[1],)), dma((COPIES[1],)),
             dma((15,)), dma((16,)), dma, dma((2,)), dma((2,)),
             dma((2, 32)), dma((2, 32)), dma, dma((2, 16)), dma((2, 16)), dma,

time: 182 us -> 175 us (0.962)
  Pallas kernels: 177 us -> 170 us
    pallas_call x1, Pallas kernels: 177 us -> 170 us  [body(): pl.pallas_call(kernel, out_shape=jax.ShapeDtypeStruct((2, 4, 49, D), BF16...]
where the time goes in v4:
time: 175 us
  Pallas kernels  170 us (97%)
  local copies, waits for them, and re-layouts  5.13 us (3%)
    pallas_call x1, Pallas kernels, body(): pl.pallas_call(kernel, out_shape=jax.ShapeDtypeStruct((2, 4, 49, D), BF16...  170 us

profile of v4, /device:TPU:35, one launch (start us, length us, event | category | flops | bytes accessed | tf_op | source)
XLA Modules:
  0.0 175.1 jit_solution(1237087054269374886)
XLA Ops:
  0.0 2.4 %copy.12 = bf16[2,1,4,49,1408]{4,3,2,0,1:T(8,128)(2,1)} copy(bf16[2,1,4,49,1408]{4,2,3,1,0:T(4,128)(2,1)} %param.11) | data formatting | bytes 2207744 | tf_op args[0]
  2.4 170.0 %shard_map.109 = bf16[2,4,49,1408]{3,2,1,0:T(8,128)(2,1)} custom-call(s32[16]{0:T(128)} %slots.1, s32[2,4]{1,0:T(2,128)} %bitcast.9, bf16[8,49,1408]{2,1,0:T(8,128)(2,1)} %bitcast.6, bf16[88,3168]{1,0:T(8,128)(2,1)} %w_qkv1.1, bf16[88,1056]{1,0:T(8,128)(2,1)} %bitcast.7, bf16[88,3168]{1,0:T(8,128)(2,1)} %w_qkv2.1, bf16[88,1056]{1,0:T(8,128)(2,1)} %bitcast.8, ...), custom_call_target="tpu_custom_call" | custom-call | flops 12000000000 | bytes 40000000 | tf_op jit(solution)/shard_map/pallas_call | solution.py:794
  172.4 2.7 %copy.13 = bf16[2,1,4,49,1408]{4,2,3,1,0:T(4,128)(2,1)} copy(bf16[2,1,4,49,1408]{4,3,2,0,1:T(8,128)(2,1)} %bitcast.5) | data formatting | bytes 2207744 | tf_op jit(solution)/shard_map/reshape | solution.py:837

commit v5 on v4

--- a/solution.py
+++ b/solution.py
@@ -424,7 +424,6 @@
 
     advance(g1)
     send_tiles((1, 3, 7, 5))
-    advance(g2)
 
     row = iota((400, 1), 0)
     last = row >= 384
@@ -466,6 +465,7 @@
         pending.append(made.wait_send)
     advance(g1)
     advance(g1)
+    advance(g2)
     for step in range(8):
         s = 4 * (step // 2) + 2 * (step % 2) + 1 - c
         tile_copy(s, 0).wait_recv()
@@ -653,7 +653,7 @@
     normalize(xw, xn, gain2, bias2, TROWS, lambda rows: jnp.logical_not(single) | (rows < 32))
     advance(g2)
     def back_copy(n, half):
-        other = lax.rem(tm + n, 16)
+        other = lax.rem(tm + jnp.where(c == 0, n, 16 - n), 16)
         return pltpu.make_async_remote_copy(
             src_ref=ret.at[half, other],
             dst_ref=obuf.at[tm, half],
@@ -664,7 +664,7 @@
         )
 
     def back_one(n):
-        other = lax.rem(tm + n, 16)
+        other = lax.rem(tm + jnp.where(c == 0, n, 16 - n), 16)
         return pltpu.make_async_remote_copy(
             src_ref=ret_one.at[pl.ds(2 * other, 2)],
             dst_ref=obuf_one.at[tm],

time: 175 us -> 175 us (level)
  the two profiles are of different devices: /device:TPU:35 before, /device:TPU:43 now
where the time goes in v5:
time: 175 us
  Pallas kernels  169 us (97%)
  local copies, waits for them, and re-layouts  5.13 us (3%)
    pallas_call x1, Pallas kernels, body(): pl.pallas_call(kernel, out_shape=jax.ShapeDtypeStruct((2, 4, 49, D), BF16...  169 us

profile of v5, /device:TPU:43, one launch (start us, length us, event | category | flops | bytes accessed | tf_op | source)
XLA Modules:
  0.0 174.6 jit_solution(727219979265866702)
XLA Ops:
  0.0 2.4 %copy.12 = bf16[2,1,4,49,1408]{4,3,2,0,1:T(8,128)(2,1)} copy(bf16[2,1,4,49,1408]{4,2,3,1,0:T(4,128)(2,1)} %param.11) | data formatting | bytes 2207744 | tf_op args[0]
  2.4 169.4 %shard_map.109 = bf16[2,4,49,1408]{3,2,1,0:T(8,128)(2,1)} custom-call(s32[16]{0:T(128)} %slots.1, s32[2,4]{1,0:T(2,128)} %bitcast.9, bf16[8,49,1408]{2,1,0:T(8,128)(2,1)} %bitcast.6, bf16[88,3168]{1,0:T(8,128)(2,1)} %w_qkv1.1, bf16[88,1056]{1,0:T(8,128)(2,1)} %bitcast.7, bf16[88,3168]{1,0:T(8,128)(2,1)} %w_qkv2.1, bf16[88,1056]{1,0:T(8,128)(2,1)} %bitcast.8, ...), custom_call_target="tpu_custom_call" | custom-call | flops 12000000000 | bytes 40000000 | tf_op jit(solution)/shard_map/pallas_call | solution.py:794
  171.9 2.7 %copy.13 = bf16[2,1,4,49,1408]{4,2,3,1,0:T(4,128)(2,1)} copy(bf16[2,1,4,49,1408]{4,3,2,0,1:T(8,128)(2,1)} %bitcast.5) | data formatting | bytes 2207744 | tf_op jit(solution)/shard_map/reshape | solution.py:837
